TPU v7x, 256 devices: a whole 4x4x8 slice. The times are simulated.
256 devices in a mesh: blk: 64 (over x_hi, z, y), head: 4 (over x_lo, core).
Axes of the slice: x: 4 (x_hi: 2, x_lo: 2; x = x_hi * 2 + x_lo), y: 4, z: 8, core: 2. Of those that a mesh axis runs over, the one named last changes fastest.
Arguments:
- queries: bfloat16 [32768, 512], P('blk', 'head'), may hold values from -6 to 6
- keys: bfloat16 [32768, 512], P('blk', 'head'), may hold values from -6 to 6
- values: bfloat16 [32768, 512], P('blk', 'head'), may hold values from -6 to 6
- out_grad: bfloat16 [32768, 512], P('blk', 'head'), may hold values from -6 to 6
- w_out: bfloat16 [512, 512], P('head'), may hold values from -0.25 to 0.25
- slot_point: int32 [64, 1024], P('blk'), may hold values from 0 to 32767, as said below
- neighbours: int32 [64, 2], P('blk'), may hold values from 0 to 63, as said below
Outputs:
- query_grad: bfloat16 [32768, 512], P('blk', 'head')
- key_grad: bfloat16 [32768, 512], P('blk', 'head')
- value_grad: bfloat16 [32768, 512], P('blk', 'head')
- w_out_grad: float32 [512, 512], P('head')
Inputs may be any that keep to these rules, and one draw needn't show every extreme that they name: `slot_point`: every entry of row p is one of the points p * 512 to p * 512 + 1023, taken modulo 32768; a point may fill several slots of a row, and some points of the range fill none. `neighbours`: row p holds 2 different patches p + o modulo 64, with o in -2 .. 2 and o not 0.
All inputs are finite; a program needn't handle non-finite values.
Results may differ from a plain program's by a relative error of at most 0.0065.
Values may be sent and summed in bfloat16 or wider, within the bound.
No kernel may reach another device: no remote copies, remote signals or barrier semaphores. Data moves between devices by JAX's collectives and lax.ppermute only.
A program may use at most 128 MiB of HBM per device.

v0:
```python
import jax
import jax.numpy as jnp
from jax import lax
from jax.sharding import PartitionSpec as P

HD = 64
REACH = 2
NB = 2


def from_behind(block, axis, distance):
    devices = range(lax.axis_size(axis))
    route = [((i - distance) % len(devices), i) for i in devices]
    return lax.ppermute(block, axis, route)


def head_backward(q_h, k_h, v_h, d_h):
    scale = 1.0 / q_h.shape[1] ** 0.5
    scores = jnp.dot(q_h, k_h.T, preferred_element_type=jnp.float32) * scale
    peak = jnp.max(scores, axis=1, keepdims=True)
    weights = jnp.exp(scores - peak)
    probs = weights / jnp.sum(weights, axis=1, keepdims=True)
    probs_low = probs.astype(jnp.bfloat16)
    attn = jnp.dot(probs_low, v_h, preferred_element_type=jnp.float32).astype(jnp.bfloat16)
    d_probs = jnp.dot(d_h, v_h.T, preferred_element_type=jnp.float32)
    delta = jnp.sum(probs * d_probs, axis=1, keepdims=True)
    d_scores = (probs * (d_probs - delta) * scale).astype(jnp.bfloat16)
    d_query = jnp.dot(d_scores, k_h, preferred_element_type=jnp.float32)
    d_key = jnp.dot(d_scores.T, q_h, preferred_element_type=jnp.float32)
    d_value = jnp.dot(probs_low.T, d_h, preferred_element_type=jnp.float32)
    return (attn, d_query, d_key, d_value)


def add_pair(first, second):
    return (first[0] + second[0], first[1] + second[1])


def local(queries, keys, values, out_grad, w_out, slot_point, neighbours):
    pts_dev, chans = queries.shape
    per_dev, span = slot_point.shape
    half = span // 2
    blocks = lax.axis_size("blk")
    place = lax.axis_index("blk")
    npts = pts_dev * blocks
    npatch = per_dev * blocks
    heads_here = chans // HD
    reach_left = (REACH + per_dev - 1) // per_dev
    reach_right = (REACH + per_dev) // per_dev
    left = [
        from_behind((keys, values, slot_point), "blk", dist) for dist in range(reach_left, 0, -1)
    ]
    right = [
        from_behind((keys, values, slot_point), "blk", -dist) for dist in range(1, reach_right + 1)
    ]
    key_win = jnp.concatenate(
        [piece[0] for piece in left] + [keys] + [piece[0] for piece in right], axis=0
    )
    value_win = jnp.concatenate(
        [piece[1] for piece in left] + [values] + [piece[1] for piece in right], axis=0
    )
    list_win = jnp.concatenate(
        [piece[2] for piece in left] + [slot_point] + [piece[2] for piece in right[:reach_left]],
        axis=0,
    )
    point_base = (place - reach_left) * pts_dev
    patch_base = (place - reach_left) * per_dev
    rim_query, rim_grad = from_behind((queries, out_grad), "blk", -1)
    query_win = jnp.concatenate([queries, rim_query], axis=0)
    grad_win = lax.all_gather(
        jnp.concatenate([out_grad, rim_grad], axis=0), "head", axis=1, tiled=True
    )
    first_point = place * pts_dev
    query_acc = jnp.zeros((pts_dev + half, chans), jnp.float32)
    key_acc = jnp.zeros((key_win.shape[0], chans), jnp.float32)
    value_acc = jnp.zeros((key_win.shape[0], chans), jnp.float32)
    weight_acc = jnp.zeros((chans, grad_win.shape[1]), jnp.float32)
    own_loc = jnp.mod(slot_point[0] - first_point, npts)
    nbr_win = jnp.mod(neighbours[0] - patch_base, npatch)
    key_lists = jnp.concatenate(
        [list_win[reach_left * per_dev]] + [list_win[nbr_win[j]] for j in range(NB)]
    )
    key_loc = jnp.mod(key_lists - point_base, npts)
    q_rows = query_win[own_loc]
    g_rows = grad_win[own_loc]
    k_rows = key_win[key_loc]
    v_rows = value_win[key_loc]
    d_attn = jnp.dot(g_rows, w_out.T, preferred_element_type=jnp.float32).astype(jnp.bfloat16)
    attn_all = []
    dq_all = []
    dk_all = []
    dv_all = []
    for head_idx in range(heads_here):
        cols = slice(head_idx * HD, (head_idx + 1) * HD)
        attn, dqh, dkh, dvh = head_backward(
            q_rows[:, cols], k_rows[:, cols], v_rows[:, cols], d_attn[:, cols]
        )
        attn_all.append(attn)
        dq_all.append(dqh)
        dk_all.append(dkh)
        dv_all.append(dvh)
    attn_rows = jnp.concatenate(attn_all, axis=1)
    weight_acc = weight_acc + jnp.dot(attn_rows.T, g_rows, preferred_element_type=jnp.float32)
    query_acc = query_acc.at[own_loc].add(jnp.concatenate(dq_all, axis=1))
    key_acc = key_acc.at[key_loc].add(jnp.concatenate(dk_all, axis=1))
    value_acc = value_acc.at[key_loc].add(jnp.concatenate(dv_all, axis=1))
    rim_back = from_behind(query_acc[pts_dev:], "blk", 1)
    query_own = query_acc[:pts_dev]
    query_own = query_own.at[:half].add(rim_back)

    def block_at(index):
        return (
            key_acc[index * pts_dev : (index + 1) * pts_dev],
            value_acc[index * pts_dev : (index + 1) * pts_dev],
        )

    total = block_at(reach_left)
    for dist in range(1, reach_left + 1):
        total = add_pair(total, from_behind(block_at(reach_left - dist), "blk", -dist))
    for dist in range(1, reach_right + 1):
        total = add_pair(total, from_behind(block_at(reach_left + dist), "blk", dist))
    weight_grad = lax.psum(weight_acc, "blk")
    return (
        query_own.astype(jnp.bfloat16),
        total[0].astype(jnp.bfloat16),
        total[1].astype(jnp.bfloat16),
        weight_grad,
    )


def solution(mesh):
    placed = (
        P("blk", "head"),
        P("blk", "head"),
        P("blk", "head"),
        P("blk", "head"),
        P("head", None),
        P("blk", None),
        P("blk", None),
    )
    return jax.shard_map(
        local,
        mesh=mesh,
        in_specs=placed,
        out_specs=(P("blk", "head"), P("blk", "head"), P("blk", "head"), P("head", None)),
        check_vma=False,
    )
```

profile of v0, /device:TPU:8, one launch (start us, length us, event | category | flops | bytes accessed | tf_op | source)
XLA Modules:
  0.0 882.8 jit_solution(15786396143831437963)
XLA Ops:
  9.5 4.2 collective-permute-start.6
  13.7 11.4 %collective-permute-start.9 = (s32[1,1024]{1,0:T(1,128)}, s32[1,1024]{1,0:T(1,128)S(1)}, u32[]{:S(2)}, u32[]{:S(2)}) collective-permute-start(s32[1,1024]{1,0:T(1,128)} %param.16), channel_id=1, source_target_pairs={{8,0},{12,4},{16,8},{20,12},{24,16},{28,20},{32,24},{36,28},{40,32... | collective-permute-start | bytes 12296 | tf_op jit(solution)/shard_map/ppermute | solution.py:14
  40.3 7.5 collective-permute-done.1
  47.8 9.1 %collective-permute-start.14 = (bf16[512,128]{1,0:T(8,128)(2,1)}, bf16[512,128]{1,0:T(8,128)(2,1)S(1)}, u32[]{:S(2)}, u32[]{:S(2)}) collective-permute-start(bf16[512,128]{1,0:T(8,128)(2,1)} %param.13), channel_id=1, source_target_pairs={{8,0},{12,4},{16,8},{20,12},{24,16},{28,20},{32,24},{36,28},{40,32... | collective-permute-start | bytes 393224 | tf_op jit(solution)/shard_map/ppermute | solution.py:14
  66.9 9.2 %gather_fusion.1 = bf16[3072,128]{1,0:T(8,128)(2,1)S(1)} fusion(bf16[3072,128]{1,0:T(8,128)(2,1)S(1)} %constant_dynamic-update-slice_fusion, s32[3072]{0:T(1024)S(1)} %broadcast_clamp_fusion), kind=kCustom, calls=%fused_computation.1 | custom fusion | bytes 1585152 | tf_op jit(solution)/shard_map/gather | solution.py:85
  76.1 6.3 multiply_reduce_fusion.3
  82.4 6.4 multiply_reduce_fusion.2
  88.8 5.7 collective-permute-start.15
  97.0 9.2 %gather_fusion.3 = bf16[3072,128]{1,0:T(8,128)(2,1)S(1)} fusion(bf16[3072,128]{1,0:T(8,128)(2,1)S(1)} %constant_dynamic-update-slice_fusion.6, s32[3072]{0:T(1024)S(1)} %broadcast_clamp_fusion), kind=kCustom, calls=%fused_computation.3 | custom fusion | bytes 1585152 | tf_op jit(solution)/shard_map/gather | solution.py:86
  106.2 7.0 fusion.1
  116.7 5.4 gather_fusion.2
  122.5 9.8 %multiply_reduce_fusion.1 = (f32[1024]{0:T(1024)S(1)}, f32[1024,3072]{1,0:T(8,128)S(1)}, f32[1024,3072]{1,0:T(8,128)}) fusion(f32[1024]{0:T(1024)S(1)} %fusion.1, f32[1024]{0:T(1024)S(1)} %get-tuple-element.45, f32[1024,3072]{1,0:T(8,128)} %get-tuple-element.46, bf16[3072,128]{1,0:T(8,128)(2,1)S(1)} %gather_fusion.3, ...), kind=kOutput, calls=%fused_computation.11 | convolution fusion | flops 418380800 | bytes 38678528 | tf_op jit(solution)/shard_map/dot_general | solution.py:25
  132.3 6.9 multiply_convert_fusion.1
  148.9 9.6 %multiply_reduce_fusion = (f32[1024]{0:T(1024)S(1)}, f32[1024,3072]{1,0:T(8,128)S(1)}, f32[1024,3072]{1,0:T(8,128)}) fusion(f32[1024]{0:T(1024)S(1)} %fusion.3, f32[1024]{0:T(1024)S(1)} %get-tuple-element.42, f32[1024,3072]{1,0:T(8,128)} %get-tuple-element.43, bf16[3072,128]{1,0:T(8,128)(2,1)S(1)} %gather_fusion.3, ...), kind=kOutput, calls=%fused_computation.8 | convolution fusion | flops 418380800 | bytes 38678528 | tf_op jit(solution)/shard_map/dot_general | solution.py:25
  163.2 7.0 multiply_convert_fusion
  178.2 17.6 %scatter_custom_fusion.1 = f32[3072,128]{1,0:T(8,128)S(1)} fusion(s32[3072]{0:T(1024)S(1)} %bitcast.20, f32[3072,128]{1,0:T(8,128)} %copy.12, f32[]{:T(128)} %constant.87.clone.1), kind=kCustom, calls=%fused_computation.34 | custom fusion | flops 393216 | bytes 1573376 | tf_op jit(solution)/shard_map/scatter-add | solution.py:104
  195.8 7.2 scatter_custom_fusion
  208.6 18.5 %scatter_custom_fusion.2 = f32[3072,128]{1,0:T(8,128)} fusion(s32[3072]{0:T(1024)S(1)} %bitcast.21, f32[3072,128]{1,0:T(8,128)} %copy.13, f32[]{:T(128)} %constant.87.clone.1), kind=kCustom, calls=%fused_computation.32 | custom fusion | flops 393216 | bytes 1573376 | tf_op jit(solution)/shard_map/scatter-add | solution.py:105
  232.5 4.2 collective-permute-start.22
  240.4 11.0 %collective-permute-start.23 = (f32[512,128]{1,0:T(8,128)S(1)}, f32[512,128]{1,0:T(8,128)S(1)}, u32[]{:S(2)}, u32[]{:S(2)}) collective-permute-start(f32[512,128]{1,0:T(8,128)S(1)} %get-tuple-element.32), channel_id=1, source_target_pairs={{8,0},{12,4},{16,8},{20,12},{24,16},{28,20},{32,24},{36,28},{40,32... | collective-permute-start | bytes 786440 | tf_op jit(solution)/shard_map/ppermute | solution.py:14
  256.4 7.5 collective-permute-start.21
  269.1 4.9 collective-permute-start.18
  275.7 7.6 collective-permute-done.20
  285.7 588.2 %all-reduce.2.cloned.1.call-done = f32[128,512]{1,0:T(8,128)} async-done(((f32[128,512]{1,0:T(8,128)}), f32[128,512]{1,0:T(8,128)}) %all-reduce.2.cloned.1.call-update) | async-done | bytes 262160 | tf_op jit(solution)/shard_map/psum | solution.py:121
  (112 shorter events, 82.7 us)
Async XLA Ops:
  7.2 109.5 %all-gather.2.cloned.1.call-start = ((), (), s32[]{:S(2)}) async-start(), calls=%async_computation | async-start | bytes 1310720 | tf_op jit(solution)/shard_map/all_gather | solution.py:69
  7.2 27.3 %collective-permute-start.8 = (s32[1,1024]{1,0:T(1,128)}, s32[1,1024]{1,0:T(1,128)S(1)}, u32[]{:S(2)}, u32[]{:S(2)}) collective-permute-start(s32[1,1024]{1,0:T(1,128)} %param.16), channel_id=1, source_target_pairs={{4,0},{8,4},{12,8},{16,12},{20,16},{24,20},{28,24},{32,28},{36,32}... | collective-permute-start | bytes 12296 | tf_op jit(solution)/shard_map/ppermute | solution.py:14
  9.5 25.1 %collective-permute-start.7 = (s32[1,1024]{1,0:T(1,128)}, s32[1,1024]{1,0:T(1,128)S(1)}, u32[]{:S(2)}, u32[]{:S(2)}) collective-permute-start(s32[1,1024]{1,0:T(1,128)} %param.16), channel_id=1, source_target_pairs={{252,0},{0,4},{4,8},{8,12},{12,16},{16,20},{20,24},{24,28},{28,32}... | collective-permute-start | bytes 12296 | tf_op jit(solution)/shard_map/ppermute | solution.py:14
  9.5 27.1 %collective-permute-start.6 = (s32[1,1024]{1,0:T(1,128)}, s32[1,1024]{1,0:T(1,128)S(1)}, u32[]{:S(2)}, u32[]{:S(2)}) collective-permute-start(s32[1,1024]{1,0:T(1,128)} %param.16), channel_id=1, source_target_pairs={{248,0},{252,4},{0,8},{4,12},{8,16},{12,20},{16,24},{20,28},{24,32... | collective-permute-start | bytes 12296 | tf_op jit(solution)/shard_map/ppermute | solution.py:14
  13.7 25.0 %collective-permute-start.9 = (s32[1,1024]{1,0:T(1,128)}, s32[1,1024]{1,0:T(1,128)S(1)}, u32[]{:S(2)}, u32[]{:S(2)}) collective-permute-start(s32[1,1024]{1,0:T(1,128)} %param.16), channel_id=1, source_target_pairs={{8,0},{12,4},{16,8},{20,12},{24,16},{28,20},{32,24},{36,28},{40,32... | collective-permute-start | bytes 12296 | tf_op jit(solution)/shard_map/ppermute | solution.py:14
  25.1 39.2 %collective-permute-start.4 = (bf16[512,128]{1,0:T(8,128)(2,1)}, bf16[512,128]{1,0:T(8,128)(2,1)S(1)}, u32[]{:S(2)}, u32[]{:S(2)}) collective-permute-start(bf16[512,128]{1,0:T(8,128)(2,1)} %param.12), channel_id=1, source_target_pairs={{8,0},{12,4},{16,8},{20,12},{24,16},{28,20},{32,24},{36,28},{40,32... | collective-permute-start | bytes 393224 | tf_op jit(solution)/shard_map/ppermute | solution.py:14
  34.5 24.5 %collective-permute-start.3 = (bf16[512,128]{1,0:T(8,128)(2,1)}, bf16[512,128]{1,0:T(8,128)(2,1)S(1)}, u32[]{:S(2)}, u32[]{:S(2)}) collective-permute-start(bf16[512,128]{1,0:T(8,128)(2,1)} %param.12), channel_id=1, source_target_pairs={{4,0},{8,4},{12,8},{16,12},{20,16},{24,20},{28,24},{32,28},{36,32}... | collective-permute-start | bytes 393224 | tf_op jit(solution)/shard_map/ppermute | solution.py:14
  34.6 23.3 %collective-permute-start.2 = (bf16[512,128]{1,0:T(8,128)(2,1)}, bf16[512,128]{1,0:T(8,128)(2,1)S(1)}, u32[]{:S(2)}, u32[]{:S(2)}) collective-permute-start(bf16[512,128]{1,0:T(8,128)(2,1)} %param.12), channel_id=1, source_target_pairs={{252,0},{0,4},{4,8},{8,12},{12,16},{16,20},{20,24},{24,28},{28,32}... | collective-permute-start | bytes 393224 | tf_op jit(solution)/shard_map/ppermute | solution.py:14
  47.8 16.6 %collective-permute-start.5 = (bf16[512,128]{1,0:T(8,128)(2,1)}, bf16[512,128]{1,0:T(8,128)(2,1)S(1)}, u32[]{:S(2)}, u32[]{:S(2)}) collective-permute-start(bf16[512,128]{1,0:T(8,128)(2,1)} %param.12), channel_id=1, source_target_pairs={{12,0},{16,4},{20,8},{24,12},{28,16},{32,20},{36,24},{40,28},{44,3... | collective-permute-start | bytes 393224 | tf_op jit(solution)/shard_map/ppermute | solution.py:14
  47.8 47.6 %collective-permute-start.14 = (bf16[512,128]{1,0:T(8,128)(2,1)}, bf16[512,128]{1,0:T(8,128)(2,1)S(1)}, u32[]{:S(2)}, u32[]{:S(2)}) collective-permute-start(bf16[512,128]{1,0:T(8,128)(2,1)} %param.13), channel_id=1, source_target_pairs={{8,0},{12,4},{16,8},{20,12},{24,16},{28,20},{32,24},{36,28},{40,32... | collective-permute-start | bytes 393224 | tf_op jit(solution)/shard_map/ppermute | solution.py:14
  57.9 37.4 %collective-permute-start.13 = (bf16[512,128]{1,0:T(8,128)(2,1)}, bf16[512,128]{1,0:T(8,128)(2,1)S(1)}, u32[]{:S(2)}, u32[]{:S(2)}) collective-permute-start(bf16[512,128]{1,0:T(8,128)(2,1)} %param.13), channel_id=1, source_target_pairs={{4,0},{8,4},{12,8},{16,12},{20,16},{24,20},{28,24},{32,28},{36,32}... | collective-permute-start | bytes 393224 | tf_op jit(solution)/shard_map/ppermute | solution.py:14
  59.0 36.3 %collective-permute-start.12 = (bf16[512,128]{1,0:T(8,128)(2,1)}, bf16[512,128]{1,0:T(8,128)(2,1)S(1)}, u32[]{:S(2)}, u32[]{:S(2)}) collective-permute-start(bf16[512,128]{1,0:T(8,128)(2,1)} %param.13), channel_id=1, source_target_pairs={{252,0},{0,4},{4,8},{8,12},{12,16},{16,20},{20,24},{24,28},{28,32}... | collective-permute-start | bytes 393224 | tf_op jit(solution)/shard_map/ppermute | solution.py:14
  64.3 31.0 %collective-permute-start.11 = (bf16[512,128]{1,0:T(8,128)(2,1)}, bf16[512,128]{1,0:T(8,128)(2,1)S(1)}, u32[]{:S(2)}, u32[]{:S(2)}) collective-permute-start(bf16[512,128]{1,0:T(8,128)(2,1)} %param.13), channel_id=1, source_target_pairs={{248,0},{252,4},{0,8},{4,12},{8,16},{12,20},{16,24},{20,28},{24,32... | collective-permute-start | bytes 393224 | tf_op jit(solution)/shard_map/ppermute | solution.py:14
  64.4 24.4 %collective-permute-start.10 = (bf16[512,128]{1,0:T(8,128)(2,1)}, bf16[512,128]{1,0:T(8,128)(2,1)S(1)}, u32[]{:S(2)}, u32[]{:S(2)}) collective-permute-start(bf16[512,128]{1,0:T(8,128)(2,1)} %param.14), channel_id=1, source_target_pairs={{4,0},{8,4},{12,8},{16,12},{20,16},{24,20},{28,24},{32,28},{36,32}... | collective-permute-start | bytes 393224 | tf_op jit(solution)/shard_map/ppermute | solution.py:14
  95.2 778.7 %all-reduce.2.cloned.1.call-start = ((), (), s32[]{:S(2)}) async-start(), calls=%async_computation.1 | async-start | bytes 524288 | tf_op jit(solution)/shard_map/psum | solution.py:121
  232.5 21.4 %collective-permute-start.22 = (f32[512,128]{1,0:T(8,128)S(1)}, f32[512,128]{1,0:T(8,128)S(1)}, u32[]{:S(2)}, u32[]{:S(2)}) collective-permute-start(f32[512,128]{1,0:T(8,128)S(1)} %get-tuple-element.28), channel_id=1, source_target_pairs={{4,0},{8,4},{12,8},{16,12},{20,16},{24,20},{28,24},{32,28},{36,32}... | collective-permute-start | bytes 786440 | tf_op jit(solution)/shard_map/ppermute | solution.py:14
  236.7 19.7 %collective-permute-start.26 = (f32[512,128]{1,0:T(8,128)S(1)}, f32[512,128]{1,0:T(8,128)S(1)}, u32[]{:S(2)}, u32[]{:S(2)}) collective-permute-start(f32[512,128]{1,0:T(8,128)S(1)} %get-tuple-element.29), channel_id=1, source_target_pairs={{244,0},{248,4},{252,8},{0,12},{4,16},{8,20},{12,24},{16,28},{20,3... | collective-permute-start | bytes 786440 | tf_op jit(solution)/shard_map/ppermute | solution.py:14
  237.3 26.5 %collective-permute-start.25 = (f32[512,128]{1,0:T(8,128)S(1)}, f32[512,128]{1,0:T(8,128)S(1)}, u32[]{:S(2)}, u32[]{:S(2)}) collective-permute-start(f32[512,128]{1,0:T(8,128)S(1)} %get-tuple-element.30), channel_id=1, source_target_pairs={{248,0},{252,4},{0,8},{4,12},{8,16},{12,20},{16,24},{20,28},{24,32... | collective-permute-start | bytes 786440 | tf_op jit(solution)/shard_map/ppermute | solution.py:14
  237.6 28.5 %collective-permute-start.24 = (f32[512,128]{1,0:T(8,128)S(1)}, f32[512,128]{1,0:T(8,128)S(1)}, u32[]{:S(2)}, u32[]{:S(2)}) collective-permute-start(f32[512,128]{1,0:T(8,128)S(1)} %get-tuple-element.31), channel_id=1, source_target_pairs={{252,0},{0,4},{4,8},{8,12},{12,16},{16,20},{20,24},{24,28},{28,32}... | collective-permute-start | bytes 786440 | tf_op jit(solution)/shard_map/ppermute | solution.py:14
  240.4 28.7 %collective-permute-start.23 = (f32[512,128]{1,0:T(8,128)S(1)}, f32[512,128]{1,0:T(8,128)S(1)}, u32[]{:S(2)}, u32[]{:S(2)}) collective-permute-start(f32[512,128]{1,0:T(8,128)S(1)} %get-tuple-element.32), channel_id=1, source_target_pairs={{8,0},{12,4},{16,8},{20,12},{24,16},{28,20},{32,24},{36,28},{40,32... | collective-permute-start | bytes 786440 | tf_op jit(solution)/shard_map/ppermute | solution.py:14
  253.9 21.8 %collective-permute-start.17 = (f32[512,128]{1,0:T(8,128)S(1)}, f32[512,128]{1,0:T(8,128)S(1)}, u32[]{:S(2)}, u32[]{:S(2)}) collective-permute-start(f32[512,128]{1,0:T(8,128)S(1)} %get-tuple-element.33), channel_id=1, source_target_pairs={{4,0},{8,4},{12,8},{16,12},{20,16},{24,20},{28,24},{32,28},{36,32}... | collective-permute-start | bytes 786440 | tf_op jit(solution)/shard_map/ppermute | solution.py:14
  256.4 19.3 %collective-permute-start.21 = (f32[512,128]{1,0:T(8,128)S(1)}, f32[512,128]{1,0:T(8,128)S(1)}, u32[]{:S(2)}, u32[]{:S(2)}) collective-permute-start(f32[512,128]{1,0:T(8,128)S(1)} %get-tuple-element.34), channel_id=1, source_target_pairs={{244,0},{248,4},{252,8},{0,12},{4,16},{8,20},{12,24},{16,28},{20,3... | collective-permute-start | bytes 786440 | tf_op jit(solution)/shard_map/ppermute | solution.py:14
  263.9 19.4 %collective-permute-start.20 = (f32[512,128]{1,0:T(8,128)S(1)}, f32[512,128]{1,0:T(8,128)S(1)}, u32[]{:S(2)}, u32[]{:S(2)}) collective-permute-start(f32[512,128]{1,0:T(8,128)S(1)} %get-tuple-element.35), channel_id=1, source_target_pairs={{248,0},{252,4},{0,8},{4,12},{8,16},{12,20},{16,24},{20,28},{24,32... | collective-permute-start | bytes 786440 | tf_op jit(solution)/shard_map/ppermute | solution.py:14
  266.1 18.9 %collective-permute-start.19 = (f32[512,128]{1,0:T(8,128)S(1)}, f32[512,128]{1,0:T(8,128)S(1)}, u32[]{:S(2)}, u32[]{:S(2)}) collective-permute-start(f32[512,128]{1,0:T(8,128)S(1)} %get-tuple-element.36), channel_id=1, source_target_pairs={{252,0},{0,4},{4,8},{8,12},{12,16},{16,20},{20,24},{24,28},{28,32}... | collective-permute-start | bytes 786440 | tf_op jit(solution)/shard_map/ppermute | solution.py:14
  (13 other events, 977.5 us)
Sparse Core Ops, SparseCore 0:
  95.3 18.8 all-gather.1
  229.4 644.4 all-reduce.1
where the time goes:
time: 894 us; the launch traced here: 883 us
  waiting for transfers between devices  610 us (68%)
  starting transfers between devices  83.8 us (9%)
  other arithmetic  76.9 us (9%)
  matrix products  53.2 us (6%)
  local copies, waits for them, and re-layouts  40.5 us (5%)
  between operations  18.8 us (2%)
    psum x1, waiting for transfers between devices, local(): weight_grad = lax.psum(weight_acc, 'blk')  588 us
    ppermute x27, starting transfers between devices, from_behind(): return lax.ppermute(block, axis, route)  83.7 us
    ppermute x27, waiting for transfers between devices, from_behind(): return lax.ppermute(block, axis, route)  21.5 us
    dot_general x2, matrix products, head_backward(): d_probs = jnp.dot(d_h, v_h.T, preferred_element_type=jnp.float32)  19.4 us
    scatter-add x1, other arithmetic, local(): value_acc = value_acc.at[key_loc].add(jnp.concatenate(dv_all, axis=1))  18.5 us
  transfers between devices with their start and end apart: 29, of which 7 were waited for; matrix products, arithmetic and copies ran while one was open for 6% of the time, Pallas kernels for 0%

commit v1 on v0

v1 whole, which is shorter than its diff:
```python
import functools

import jax
import jax.numpy as jnp
from jax import lax
from jax.experimental import pallas as pl
from jax.experimental.pallas import tpu as pltpu
from jax.sharding import PartitionSpec as P

HD = 64
BLK = 512
WIN = 6 * BLK
TILE = 256
META = 32
UNIT = 2 * BLK + META
PLANES = 16
AXES = ("blk", "head")
F32 = jnp.float32
BF16 = jnp.bfloat16
ABSENT = -1e30


def device_id(plane, y, x, core):
    return ((plane % PLANES) * 4 + y % 4) * 4 + x * 2 + core


def send(block, target):
    route = []
    for plane in range(PLANES):
        for y in range(4):
            for x in range(2):
                for core in range(2):
                    there = target(plane, y, x, core)
                    if there is not None:
                        route.append((device_id(plane, y, x, core), device_id(*there)))
    return lax.ppermute(block, AXES, route)


def contract(a, b, dim_a, dim_b):
    return lax.dot_general(
        a, b, (((dim_a,), (dim_b,)), ((), ())), preferred_element_type=F32
    )


def attention_kernel(
    place_ref, plane_ref, left_ref, right_ref, last_ref,
    plane_out, edge_out, rows_out,
    kv, query, cot, meta, bias, weight, kv_acc, row_acc,
):
    core = place_ref[0]
    y = place_ref[1]

    def plane_rows(block, start, count):
        base = lax.rem(block - y + 4, 4) * UNIT + start
        return plane_ref[pl.ds(pl.multiple_of(base, META), count), :]

    lane = lax.broadcasted_iota(jnp.int32, (BLK, 2 * HD), 1)

    def put_query(slot, rows):
        zero = jnp.zeros_like(rows)
        at = pl.ds(slot * BLK, BLK)
        query[at, :] = jnp.where(lane < HD, rows * 0.125, zero)
        cot[at, :] = jnp.where(lane < HD, zero, rows)

    @pl.when(core == 0)
    def _():
        kv[0 : 2 * BLK, :] = left_ref[0 : 2 * BLK, :]
        kv[6 * BLK : 7 * BLK, :] = last_ref[...]
        meta[0 : 2 * META, :] = left_ref[2 * BLK : 2 * BLK + 2 * META, :]
        for block in range(4):
            kv[(2 + block) * BLK : (3 + block) * BLK, :] = plane_rows(block, 0, BLK)
            meta[(2 + block) * META : (3 + block) * META, :] = plane_rows(block, 2 * BLK, META)
        for slot in range(3):
            put_query(slot, plane_rows(slot, BLK, BLK))

    @pl.when(core == 1)
    def _():
        kv[4 * BLK : 7 * BLK, :] = right_ref[0 : 3 * BLK, :]
        meta[4 * META : 6 * META, :] = right_ref[4 * BLK : 4 * BLK + 2 * META, :]
        for block in range(4):
            kv[block * BLK : (1 + block) * BLK, :] = plane_rows(block, 0, BLK)
            meta[block * META : (1 + block) * META, :] = plane_rows(block, 2 * BLK, META)
        for slot in range(2):
            put_query(slot, plane_rows(2 + slot, BLK, BLK))
        put_query(2, right_ref[3 * BLK : 4 * BLK, :])

    def counts(patch):
        rows = meta[patch * META : (patch + 1) * META, :].astype(F32)
        return rows[0:8, :] * 32.0 + rows[8:16, :]

    eye = lax.broadcasted_iota(jnp.int32, (128, 128), 0) == lax.broadcasted_iota(
        jnp.int32, (128, 128), 1
    )
    for job in range(2):
        near = meta[(2 + job) * META + 16 : (2 + job) * META + 32, :].astype(F32)[0:1, :]

        def chosen(patch, near=near, job=job):
            if patch < 0 or patch > 5:
                return None
            if patch == 2 + job:
                return jnp.ones((1, 1), F32)
            offset = float(patch - 2 - job)
            hit = (near[:, 0:1] == offset) | (near[:, 1:2] == offset)
            return hit.astype(F32)

        for block in range(6):
            slot = block + job
            total = jnp.zeros((4, 128), F32)
            if abs(slot - 2 - job) <= 2 and slot <= 5:
                total = total + counts(slot)[0:4, :] * chosen(slot)
            if abs(slot - 3 - job) <= 2 and slot >= 1:
                total = total + counts(slot - 1)[4:8, :] * chosen(slot - 1)
            logs = jnp.where(total > 0.5, jnp.log(jnp.maximum(total, 1.0)), ABSENT)
            for row in range(4):
                at = block * BLK + row * 128
                bias[job, 0:1, at : at + 128] = logs[row : row + 1, :]
        own = counts(2 + job)
        for row in range(8):
            spread = jnp.where(eye, jnp.broadcast_to(own[row : row + 1, :], (128, 128)), 0.0)
            weight[job, row * 128 : (row + 1) * 128, :] = jnp.sum(spread, axis=1, keepdims=True)

    kv_acc[...] = jnp.zeros_like(kv_acc)
    row_acc[...] = jnp.zeros_like(row_acc)
    tile_lane = lax.broadcasted_iota(jnp.int32, (TILE, 2 * HD), 1)

    for job in range(2):

        def step(tile, carry, job=job):
            first = job * BLK
            keys = kv[first : first + WIN, :]
            rows = pl.ds(pl.multiple_of(first + tile * TILE, TILE), TILE)
            q = query[rows, :]
            d = cot[rows, :]
            times = weight[job, pl.ds(pl.multiple_of(tile * TILE, TILE), TILE), :]
            scores = contract(q, keys, 1, 1) + bias[job]
            peak = jnp.max(scores, axis=1, keepdims=True)
            grown = jnp.exp(scores - peak)
            probs = grown * (times / jnp.sum(grown, axis=1, keepdims=True))
            probs_low = probs.astype(BF16)
            attn = contract(probs_low, keys, 1, 0)
            d_probs = contract(d, keys, 1, 1)
            delta = jnp.sum(attn * d.astype(F32), axis=1, keepdims=True) / jnp.maximum(times, 1.0)
            d_scores = (probs * (d_probs - delta)).astype(BF16)
            d_query = contract(d_scores, keys, 1, 0) * 0.125
            row_acc[rows, :] += jnp.where(tile_lane < HD, d_query, attn)
            kv_acc[:, first : first + WIN] += contract(q, d_scores, 0, 0) + contract(
                d, probs_low, 0, 0
            )
            return carry

        lax.fori_loop(0, 2 * BLK // TILE, step, 0)

    rows_out[...] = row_acc[...].astype(BF16)

    def grads(slot):
        return kv_acc[:, slot * BLK : (slot + 1) * BLK].T.astype(BF16)

    edge_out[3 * BLK : 4 * BLK, :] = row_acc[2 * BLK : 3 * BLK, :].astype(BF16)

    @pl.when(core == 0)
    def _():
        for block in range(4):
            plane_out[block * BLK : (block + 1) * BLK, :] = grads(2 + block)
        for place, slot in enumerate((0, 1, 6)):
            edge_out[place * BLK : (place + 1) * BLK, :] = grads(slot)

    @pl.when(core == 1)
    def _():
        for block in range(4):
            plane_out[block * BLK : (block + 1) * BLK, :] = grads(block)
        for place, slot in enumerate((4, 5, 6)):
            edge_out[place * BLK : (place + 1) * BLK, :] = grads(slot)


def attention(place, plane, left, right, last):
    vmem = pl.BlockSpec(memory_space=pltpu.VMEM)
    return pl.pallas_call(
        attention_kernel,
        out_shape=(
            jax.ShapeDtypeStruct((4 * BLK, 2 * HD), BF16),
            jax.ShapeDtypeStruct((4 * BLK, 2 * HD), BF16),
            jax.ShapeDtypeStruct((3 * BLK, 2 * HD), BF16),
        ),
        in_specs=[pl.BlockSpec(memory_space=pltpu.SMEM)] + [vmem] * 4,
        out_specs=(vmem, vmem, vmem),
        scratch_shapes=[
            pltpu.VMEM((7 * BLK, 2 * HD), BF16),
            pltpu.VMEM((3 * BLK, 2 * HD), BF16),
            pltpu.VMEM((3 * BLK, 2 * HD), BF16),
            pltpu.VMEM((6 * META, 2 * HD), BF16),
            pltpu.VMEM((2, 1, WIN), F32),
            pltpu.VMEM((2, 2 * BLK, 1), F32),
            pltpu.VMEM((2 * HD, 7 * BLK), F32),
            pltpu.VMEM((3 * BLK, 2 * HD), F32),
        ],
        compiler_params=pltpu.CompilerParams(vmem_limit_bytes=56 * 1024 * 1024),
        cost_estimate=pl.CostEstimate(
            flops=40_000_000_000, bytes_accessed=4_000_000, transcendentals=6_300_000
        ),
        name="attention_backward",
    )(place, plane, left, right, last)


def local(queries, keys, values, out_grad, w_out, slot_point, neighbours):
    place = lax.axis_index("blk")
    head = lax.axis_index("head")
    y = lax.rem(place, 4)
    core = lax.rem(head, 2)
    anchor = y // 2
    npts = BLK * lax.axis_size("blk")
    blocks = lax.axis_size("blk")

    with jax.named_scope("cotangent"):
        grad_all = lax.all_gather(out_grad, "head", axis=1, tiled=True)
        d_attn = jnp.dot(grad_all, w_out.T, preferred_element_type=F32).astype(BF16)

    with jax.named_scope("units"):
        slots = jnp.mod(slot_point[0] - place * BLK, npts)
        bins = lax.broadcasted_iota(jnp.int32, (2 * BLK, 2 * BLK), 1)
        count = jnp.sum((slots[:, None] == bins).astype(jnp.int32), axis=0)
        offset = jnp.mod(neighbours[0] - place + blocks // 2, blocks) - blocks // 2
        near = jnp.pad(offset[None, :], ((0, 15), (0, 126)))
        meta = jnp.concatenate(
            [(count // 32).reshape(8, 128), (count % 32).reshape(8, 128), near]
        ).astype(BF16)

        def unit(j):
            cols = slice(j * HD, (j + 1) * HD)
            return jnp.concatenate(
                [
                    jnp.concatenate([keys[:, cols], values[:, cols]], axis=1),
                    jnp.concatenate([queries[:, cols], d_attn[:, cols]], axis=1),
                    meta,
                ]
            )

        units = (unit(0), unit(1))
        odd = lax.rem(y, 2) == 1
        same = jnp.where(odd, units[1], units[0])
        other = jnp.where(odd, units[0], units[1])

    def along_y(hops):
        def target(plane, y, x, core):
            there = (y + hops) % 4
            return (plane, there, x, core) if there // 2 == core else None

        return target

    with jax.named_scope("gather_y"):
        got = [send(same if k == 2 else other, along_y(k)) for k in (1, 2, 3)]
        held = jnp.concatenate([same, got[2], got[1], got[0]])

    with jax.named_scope("gather_z"):

        def held_unit(block):
            return lax.dynamic_slice_in_dim(held, lax.rem(block - y + 4, 4) * UNIT, UNIT, 0)

        first, second, third, fourth = [held_unit(i) for i in range(4)]
        kv_rows = slice(0, BLK)
        query_rows = slice(BLK, 2 * BLK)
        meta_rows = slice(2 * BLK, UNIT)
        from_left = jnp.concatenate(
            [third[kv_rows], fourth[kv_rows], third[meta_rows], fourth[meta_rows]]
        )
        from_right = jnp.concatenate(
            [
                first[kv_rows], second[kv_rows], third[kv_rows], first[query_rows],
                first[meta_rows], second[meta_rows],
            ]
        )
        shared = send(held, lambda p, y, x, c: (p, y, x, 1 - c) if c == y // 2 else None)
        left = send(from_left, lambda p, y, x, c: (p + 1, y, x, 0) if c == y // 2 else None)
        right = send(from_right, lambda p, y, x, c: (p - 1, y, x, 1) if c == y // 2 else None)
        last = send(first[kv_rows], lambda p, y, x, c: (p - 1, y, x, 0) if c == y // 2 else None)
        is_anchor = core == anchor
        plane = jnp.where(is_anchor, held, shared)

    with jax.named_scope("spread_grad"):
        grad_sent, plane, left, right, last = lax.optimization_barrier(
            (grad_all, plane, left, right, last)
        )

        def grad_target(hops):
            def target(p, y, x, c):
                if c == 0:
                    return (p, y + hops, x, c) if hops and y <= 2 else None
                if y == 0:
                    return (p - 1, hops, x, c)
                return (p, y + hops, x, c) if hops and y >= 2 else None

            return target

        grads = [send(grad_sent, grad_target(k)) for k in range(4)]

    with jax.named_scope("attention"):
        where = jnp.stack([core, y]).astype(jnp.int32)
        plane_grad, edge_grad, row_grad = attention(where, plane, left, right, last)

    with jax.named_scope("w_out_grad"):

        def attn_block(index):
            at = jnp.clip(index, 0, 2) * BLK
            return lax.dynamic_slice(row_grad, (at, HD), (BLK, HD))

        def part(index, grad):
            return lax.dot_general(
                attn_block(index), grad, (((0,), (0,)), ((), ())), preferred_element_type=F32
            )

        own_valid = jnp.where(core == 0, y <= 2, y >= 2)
        w_part = part(y - 2 * core, jnp.where(own_valid, grad_all, jnp.zeros_like(grad_all)))
        for k in range(4):
            index = jnp.where(
                core == 0,
                lax.rem(y - k + 4, 4),
                jnp.where(y == k, 2, lax.rem(y - k + 4, 4) - 2),
            )
            w_part = w_part + part(index, grads[k])
        w_low = w_part.astype(BF16)

    with jax.named_scope("return_z"):
        to_anchor = lambda p, y, x, c: (p, y, x, y // 2) if c != y // 2 else None
        w_pair = send(w_low, lambda p, y, x, c: (p, y, x, 1 - c))
        back_plane = send(plane_grad, to_anchor)
        back_rows = send(row_grad, to_anchor)
        back_right = send(
            edge_grad, lambda p, y, x, c: (p + 1, y, x, y // 2) if c == 1 else None
        )
        back_left = send(
            edge_grad[: 2 * BLK], lambda p, y, x, c: (p - 1, y, x, y // 2) if c == 0 else None
        )
        back_last = send(
            edge_grad[2 * BLK : 3 * BLK],
            lambda p, y, x, c: (p + 1, y, x, y // 2) if c == 0 else None,
        )

    with jax.named_scope("reduce_w"):
        w_sum = w_low.astype(F32) + w_pair.astype(F32)
        for stride in (1, 4):
            w_low = w_sum.astype(BF16)
            others = [
                send(w_low, lambda p, y, x, c, k=k: (p ^ (k * stride), y, x, c))
                for k in (1, 2, 3)
            ]
            w_sum = (w_low.astype(F32) + others[0].astype(F32)) + (
                others[1].astype(F32) + others[2].astype(F32)
            )
        w_low = w_sum.astype(BF16)

    with jax.named_scope("return_y"):
        plane_total = plane_grad.astype(F32) + back_plane.astype(F32)
        right_f = back_right.astype(F32)
        zero = jnp.zeros((BLK, 2 * HD), F32)
        plane_total = plane_total + jnp.concatenate(
            [right_f[:BLK] + back_last.astype(F32), right_f[BLK : 3 * BLK], zero]
        )
        plane_total = plane_total + jnp.concatenate([zero, zero, back_left.astype(F32)])
        low = jnp.where(core == 0, row_grad, back_rows).astype(F32)
        high = jnp.where(core == 0, back_rows, row_grad).astype(F32)
        rows_total = jnp.concatenate(
            [
                low[:BLK] + right_f[3 * BLK :],
                low[BLK : 2 * BLK],
                low[2 * BLK :] + high[:BLK],
                high[BLK : 2 * BLK],
            ]
        )
        result = jnp.concatenate(
            [
                plane_total.astype(BF16).reshape(4, BLK, 2 * HD),
                rows_total.astype(BF16).reshape(4, BLK, 2 * HD),
            ],
            axis=1,
        )

        def result_at(index):
            return lax.dynamic_index_in_dim(result, lax.rem(index, 4), 0, keepdims=False)

        def from_anchor(hops):
            return lambda p, y, x, c: (p, y + hops, x, c) if c == y // 2 else None

        parts = [result_at(y)] + [send(result_at(y + k), from_anchor(k)) for k in (1, 2, 3)]
        w_parts = [w_low] + [send(w_low, from_anchor(k)) for k in (1, 2, 3)]
        parts = jnp.stack(parts)
        w_parts = jnp.stack(w_parts)

        def head_part(stack, j):
            return lax.dynamic_index_in_dim(
                stack, lax.rem(y - 2 * core - j + 4, 4), 0, keepdims=False
            )

        heads = [head_part(parts, j) for j in range(2)]
        d_key = jnp.concatenate([u[:BLK, :HD] for u in heads], axis=1)
        d_value = jnp.concatenate([u[:BLK, HD:] for u in heads], axis=1)
        d_query = jnp.concatenate([u[BLK:, :HD] for u in heads], axis=1)
        w_grad = jnp.concatenate([head_part(w_parts, j) for j in range(2)]).astype(F32)
    return d_query, d_key, d_value, w_grad


def solution(mesh):
    placed = (
        P("blk", "head"),
        P("blk", "head"),
        P("blk", "head"),
        P("blk", "head"),
        P("head", None),
        P("blk", None),
        P("blk", None),
    )
    return jax.shard_map(
        local,
        mesh=mesh,
        in_specs=placed,
        out_specs=(P("blk", "head"), P("blk", "head"), P("blk", "head"), P("head", None)),
        check_vma=False,
    )
```

time: 894 us -> 152 us (0.17); the launches traced: 883 us -> 150 us
  waiting for transfers between devices: 610 us -> 22.9 us
  other arithmetic: 76.9 us -> 7.07 us
  matrix products: 53.2 us -> 2.73 us
  local copies, waits for them, and re-layouts: 40.5 us -> 7.75 us
  Pallas kernels: 0 us -> 28.2 us
  between operations: 18.8 us -> 1.56 us
  starting transfers between devices: 83.8 us -> 72.4 us
    psum x1 -> x0, waiting for transfers between devices: 588 us -> none  [local(): weight_grad = lax.psum(weight_acc, 'blk')]
    dot_general x14 -> x6, matrix products: 53.2 us -> 2.73 us  [the longest x5 2.43 us: part(): lax.dot_general(attn_block(index), grad, (((0,), (0,)), ((), ())), prefer...]
    scatter-add x3 -> x0, other arithmetic: 43.3 us -> none  [the longest x1 18.5 us: local(): value_acc = value_acc.at[key_loc].add(jnp.concatenate(dv_all, axis=1))]
    pallas_call x0 -> x1, Pallas kernels: none -> 28.2 us  [attention(): pl.pallas_call(attention_kernel, out_shape=(jax.ShapeDtypeStruct((4 * BLK...]
    gather x4 -> x0, local copies, waits for them, and re-layouts: 26.9 us -> none  [the longest x1 9.16 us: local(): k_rows = key_win[key_loc]]
    convert_element_type x5 -> x7, other arithmetic: 17 us -> 1.36 us  [the longest x1 0.73 us: local(): jnp.concatenate([head_part(w_parts, j) for j in range(2)]).astype(F32)]
    ppermute x27 -> x29, starting transfers between devices: 83.7 us -> 72.4 us  [send(): return lax.ppermute(block, AXES, route)]
    ppermute x27 -> x29, waiting for transfers between devices: 21.5 us -> 22.9 us  [send(): return lax.ppermute(block, AXES, route)]
  transfers between devices with their start and end apart: 29 -> 29, of which waited for: 7 -> 9; matrix products, arithmetic and copies ran while one was open for 6% -> 7% of each run, Pallas kernels for 0% -> 0%
where the time goes in v1:
time: 152 us; the launch traced here: 150 us
  starting transfers between devices  72.4 us (48%)
  Pallas kernels  28.2 us (19%)
  waiting for transfers between devices  22.9 us (15%)
  local copies, waits for them, and re-layouts  7.75 us (5%)
  blocking collectives  7.33 us (5%)
  other arithmetic  7.07 us (5%)
  matrix products  2.73 us (2%)
  between operations  1.56 us (1%)
    ppermute x29, starting transfers between devices, send(): return lax.ppermute(block, AXES, route)  72.4 us
    pallas_call x1, Pallas kernels, attention(): pl.pallas_call(attention_kernel, out_shape=(jax.ShapeDtypeStruct((4 * BLK...  28.2 us
    ppermute x29, waiting for transfers between devices, send(): return lax.ppermute(block, AXES, route)  22.9 us
    all_gather x1, blocking collectives, local(): grad_all = lax.all_gather(out_grad, 'head', axis=1, tiled=True)  7.33 us
    unnamed x34, local copies, waits for them, and re-layouts  3.04 us
  transfers between devices with their start and end apart: 29, of which 9 were waited for; matrix products, arithmetic and copies ran while one was open for 7% of the time, Pallas kernels for 0%

profile of v1, /device:TPU:8, one launch (start us, length us, event | category | flops | bytes accessed | tf_op | source)
XLA Modules:
  0.0 149.9 jit_solution(5422722818719467788)
XLA Ops:
  2.9 7.3 %all_gather.3 = bf16[512,512]{1,0:T(8,128)(2,1)S(1)} all-gather(bf16[512,128]{1,0:T(8,128)(2,1)S(1)} %copy-done.9), channel_id=1, replica_groups=mesh['blk'=64,'head'=4] {'head'}, dimensions={1}, use_global_device_ids=true | all-gather | bytes 655360 | tf_op jit(solution)/shard_map/cotangent/all_gather | solution.py:214
  12.0 3.4 %collective-permute-start = (bf16[1056,128]{1,0:T(8,128)(2,1)S(1)}, bf16[1056,128]{1,0:T(8,128)(2,1)S(1)}, u32[]{:S(2)}, u32[]{:S(2)}) collective-permute-start(bf16[1056,128]{1,0:T(8,128)(2,1)S(1)} %get-tuple-element.41), channel_id=1, source_target_pairs={{1,13},{3,15},{4,0},{6,2},{8,4},{10,6},{13,9},{15,11},{17,29},{19,... | collective-permute-start | bytes 811016 | tf_op jit(solution)/shard_map/gather_y/ppermute | solution.py:36
  18.1 2.3 %collective-permute-done = bf16[1056,128]{1,0:T(8,128)(2,1)S(1)} collective-permute-done((bf16[1056,128]{1,0:T(8,128)(2,1)S(1)}, bf16[1056,128]{1,0:T(8,128)(2,1)S(1)}, u32[]{:S(2)}, u32[]{:S(2)}) %collective-permute-start) | collective-permute-done | bytes 270368 | tf_op jit(solution)/shard_map/gather_y/ppermute | solution.py:36
  20.4 4.9 %collective-permute-done.1 = bf16[1056,128]{1,0:T(8,128)(2,1)S(1)} collective-permute-done((bf16[1056,128]{1,0:T(8,128)(2,1)S(1)}, bf16[1056,128]{1,0:T(8,128)(2,1)S(1)}, u32[]{:S(2)}, u32[]{:S(2)}) %collective-permute-start.1) | collective-permute-done | bytes 270368 | tf_op jit(solution)/shard_map/gather_y/ppermute | solution.py:36
  29.1 3.4 %collective-permute-start.4 = (bf16[1088,128]{1,0:T(8,128)(2,1)S(1)}, bf16[1088,128]{1,0:T(8,128)(2,1)S(1)}, u32[]{:S(2)}, u32[]{:S(2)}) collective-permute-start(bf16[1088,128]{1,0:T(8,128)(2,1)S(1)} %pad_maximum_fusion.3), channel_id=1, source_target_pairs={{0,16},{2,18},{4,20},{6,22},{9,24},{11,26},{13,28},{15,30},{16,32}... | collective-permute-start | bytes 835592 | tf_op jit(solution)/shard_map/gather_z/ppermute | solution.py:36
  32.4 5.5 %collective-permute-start.5 = (bf16[2112,128]{1,0:T(8,128)(2,1)S(1)}, bf16[2112,128]{1,0:T(8,128)(2,1)S(1)}, u32[]{:S(2)}, u32[]{:S(2)}) collective-permute-start(bf16[2112,128]{1,0:T(8,128)(2,1)S(1)} %get-tuple-element.26), channel_id=1, source_target_pairs={{0,241},{2,243},{4,245},{6,247},{9,249},{11,251},{13,253},{15,255}... | collective-permute-start | bytes 1622024 | tf_op jit(solution)/shard_map/gather_z/ppermute | solution.py:36
  38.0 3.8 %collective-permute-start.6 = (bf16[512,128]{1,0:T(8,128)(2,1)S(1)}, bf16[512,128]{1,0:T(8,128)(2,1)S(1)}, u32[]{:S(2)}, u32[]{:S(2)}) collective-permute-start(bf16[512,128]{1,0:T(8,128)(2,1)S(1)} %get-tuple-element.25), channel_id=1, source_target_pairs={{0,240},{2,242},{4,244},{6,246},{9,248},{11,250},{13,252},{15,254}... | collective-permute-start | bytes 393224 | tf_op jit(solution)/shard_map/gather_z/ppermute | solution.py:36
  43.2 3.0 %collective-permute-done.6.last_ref = bf16[512,128]{1,0:T(8,128)(2,1)S(1)} collective-permute-done((bf16[512,128]{1,0:T(8,128)(2,1)S(1)}, bf16[512,128]{1,0:T(8,128)(2,1)S(1)}, u32[]{:S(2)}, u32[]{:S(2)}) %collective-permute-start.6) | collective-permute-done | bytes 131104 | tf_op jit(solution)/shard_map/gather_z/ppermute | solution.py:36
  47.8 28.2 %attention_backward.1 = (bf16[2048,128]{1,0:T(8,128)(2,1)}, bf16[2048,128]{1,0:T(8,128)(2,1)}, bf16[1536,128]{1,0:T(8,128)(2,1)}) custom-call(s32[2]{0:T(128)} %pad_add_fusion.place_ref, bf16[4224,128]{1,0:T(8,128)(2,1)} %broadcast_select_fusion.plane_ref, bf16[1088,128]{1,0:T(8,128)(2,1)} %copy-done.12, bf16[2112,128]{1,0:T(8,128)(2,1)} %copy-done.11, ...), custom_call_target="tpu_custom_call" | custom-call | flops 40000000000 | bytes 4000000 | tf_op jit(solution)/shard_map/attention/attention_backward/pallas_call | solution.py:177
  78.3 4.7 %collective-permute-start.17 = (bf16[512,512]{1,0:T(8,128)(2,1)S(1)}, bf16[512,512]{1,0:T(8,128)(2,1)S(1)}, u32[]{:S(2)}, u32[]{:S(2)}) collective-permute-start(bf16[512,512]{1,0:T(8,128)(2,1)S(1)} %all_gather.3), channel_id=1, source_target_pairs={{0,8},{1,249},{2,10},{3,251},{4,12},{6,14},{8,0},{9,1},{10,2},{11,... | collective-permute-start | bytes 1572872 | tf_op jit(solution)/shard_map/spread_grad/ppermute | solution.py:36
  83.0 4.2 %collective-permute-start.18 = (bf16[512,512]{1,0:T(8,128)(2,1)S(1)}, bf16[512,512]{1,0:T(8,128)(2,1)S(1)}, u32[]{:S(2)}, u32[]{:S(2)}) collective-permute-start(bf16[512,512]{1,0:T(8,128)(2,1)S(1)} %all_gather.3), channel_id=1, source_target_pairs={{0,12},{1,253},{2,14},{3,255},{4,0},{6,2},{8,4},{9,5},{10,6},{11,7... | collective-permute-start | bytes 1572872 | tf_op jit(solution)/shard_map/spread_grad/ppermute | solution.py:36
  87.2 1.9 %collective-permute-start.16 = (bf16[512,512]{1,0:T(8,128)(2,1)S(1)}, bf16[512,512]{1,0:T(8,128)(2,1)S(1)}, u32[]{:S(2)}, u32[]{:S(2)}) collective-permute-start(bf16[512,512]{1,0:T(8,128)(2,1)S(1)} %all_gather.3), channel_id=1, source_target_pairs={{0,4},{1,245},{2,6},{3,247},{4,8},{6,10},{8,12},{9,13},{10,14},{11... | collective-permute-start | bytes 1572872 | tf_op jit(solution)/shard_map/spread_grad/ppermute | solution.py:36
  93.9 2.1 %collective-permute-start.9 = (bf16[512,128]{1,0:T(8,128)(2,1)S(1)}, bf16[512,128]{1,0:T(8,128)(2,1)S(1)}, u32[]{:S(2)}, u32[]{:S(2)}) collective-permute-start(bf16[512,128]{1,0:T(8,128)(2,1)S(1)} %slice.122), channel_id=1, source_target_pairs={{0,16},{2,18},{4,20},{6,22},{8,25},{10,27},{12,29},{14,31},{16,32}... | collective-permute-start | bytes 393224 | tf_op jit(solution)/shard_map/return_z/ppermute | solution.py:36
  96.3 7.5 %collective-permute-start.10 = (bf16[1024,128]{1,0:T(8,128)(2,1)S(1)}, bf16[1024,128]{1,0:T(8,128)(2,1)S(1)}, u32[]{:S(2)}, u32[]{:S(2)}) collective-permute-start(bf16[1024,128]{1,0:T(8,128)(2,1)S(1)} %slice.124), channel_id=1, source_target_pairs={{0,240},{2,242},{4,244},{6,246},{8,249},{10,251},{12,253},{14,255}... | collective-permute-start | bytes 786440 | tf_op jit(solution)/shard_map/return_z/ppermute | solution.py:36
  105.8 3.5 %collective-permute-done.16 = bf16[512,512]{1,0:T(8,128)(2,1)S(1)} collective-permute-done((bf16[512,512]{1,0:T(8,128)(2,1)S(1)}, bf16[512,512]{1,0:T(8,128)(2,1)S(1)}, u32[]{:S(2)}, u32[]{:S(2)}) %collective-permute-start.16) | collective-permute-done | bytes 524320 | tf_op jit(solution)/shard_map/spread_grad/ppermute | solution.py:36
  111.9 3.4 %collective-permute-start.21 = (bf16[64,512]{1,0:T(8,128)(2,1)S(1)}, bf16[64,512]{1,0:T(8,128)(2,1)S(1)}, u32[]{:S(2)}, u32[]{:S(2)}) collective-permute-start(bf16[64,512]{1,0:T(8,128)(2,1)S(1)} %add_convert_fusion.2), channel_id=1, source_target_pairs={{0,32},{1,33},{2,34},{3,35},{4,36},{5,37},{6,38},{7,39},{8,40},{9,... | collective-permute-start | bytes 196616 | tf_op jit(solution)/shard_map/reduce_w/ppermute | solution.py:36
  115.5 3.9 %collective-permute-done.21 = bf16[64,512]{1,0:T(8,128)(2,1)S(1)} collective-permute-done((bf16[64,512]{1,0:T(8,128)(2,1)S(1)}, bf16[64,512]{1,0:T(8,128)(2,1)S(1)}, u32[]{:S(2)}, u32[]{:S(2)}) %collective-permute-start.21) | collective-permute-done | bytes 65568 | tf_op jit(solution)/shard_map/reduce_w/ppermute | solution.py:36
  119.4 2.0 %collective-permute-done.22 = bf16[64,512]{1,0:T(8,128)(2,1)S(1)} collective-permute-done((bf16[64,512]{1,0:T(8,128)(2,1)S(1)}, bf16[64,512]{1,0:T(8,128)(2,1)S(1)}, u32[]{:S(2)}, u32[]{:S(2)}) %collective-permute-start.22) | collective-permute-done | bytes 65568 | tf_op jit(solution)/shard_map/reduce_w/ppermute | solution.py:36
  121.5 4.3 %collective-permute-start.23 = (bf16[64,512]{1,0:T(8,128)(2,1)S(1)}, bf16[64,512]{1,0:T(8,128)(2,1)S(1)}, u32[]{:S(2)}, u32[]{:S(2)}) collective-permute-start(bf16[64,512]{1,0:T(8,128)(2,1)S(1)} %add_convert_fusion.1), channel_id=1, source_target_pairs={{0,64},{1,65},{2,66},{3,67},{4,68},{5,69},{6,70},{7,71},{8,72},{9,... | collective-permute-start | bytes 196616 | tf_op jit(solution)/shard_map/reduce_w/ppermute | solution.py:36
  125.8 2.7 %collective-permute-start.24 = (bf16[64,512]{1,0:T(8,128)(2,1)S(1)}, bf16[64,512]{1,0:T(8,128)(2,1)S(1)}, u32[]{:S(2)}, u32[]{:S(2)}) collective-permute-start(bf16[64,512]{1,0:T(8,128)(2,1)S(1)} %add_convert_fusion.1), channel_id=1, source_target_pairs={{0,128},{1,129},{2,130},{3,131},{4,132},{5,133},{6,134},{7,135},{8... | collective-permute-start | bytes 196616 | tf_op jit(solution)/shard_map/reduce_w/ppermute | solution.py:36
  128.5 1.9 %collective-permute-start.25 = (bf16[64,512]{1,0:T(8,128)(2,1)S(1)}, bf16[64,512]{1,0:T(8,128)(2,1)S(1)}, u32[]{:S(2)}, u32[]{:S(2)}) collective-permute-start(bf16[64,512]{1,0:T(8,128)(2,1)S(1)} %add_convert_fusion.1), channel_id=1, source_target_pairs={{0,192},{1,193},{2,194},{3,195},{4,196},{5,197},{6,198},{7,199},{8... | collective-permute-start | bytes 196616 | tf_op jit(solution)/shard_map/reduce_w/ppermute | solution.py:36
  134.3 2.6 %collective-permute-start.13 = (bf16[1024,128]{1,0:T(8,128)(2,1)S(1)}, bf16[1024,128]{1,0:T(8,128)(2,1)S(1)}, u32[]{:S(2)}, u32[]{:S(2)}) collective-permute-start(bf16[1024,128]{1,0:T(8,128)(2,1)S(1)} %get-tuple-element.34), channel_id=1, source_target_pairs={{0,8},{2,10},{4,12},{6,14},{9,1},{11,3},{13,5},{15,7},{16,24},{18,... | collective-permute-start | bytes 786440 | tf_op jit(solution)/shard_map/return_y/ppermute | solution.py:36
  136.9 2.3 %collective-permute-done.25 = bf16[64,512]{1,0:T(8,128)(2,1)S(1)} collective-permute-done((bf16[64,512]{1,0:T(8,128)(2,1)S(1)}, bf16[64,512]{1,0:T(8,128)(2,1)S(1)}, u32[]{:S(2)}, u32[]{:S(2)}) %collective-permute-start.25) | collective-permute-done | bytes 65568 | tf_op jit(solution)/shard_map/reduce_w/ppermute | solution.py:36
  142.5 3.9 %collective-permute-start.28 = (bf16[64,512]{1,0:T(8,128)(2,1)S(1)}, bf16[64,512]{1,0:T(8,128)(2,1)S(1)}, u32[]{:S(2)}, u32[]{:S(2)}) collective-permute-start(bf16[64,512]{1,0:T(8,128)(2,1)S(1)} %add_convert_fusion), channel_id=1, source_target_pairs={{0,12},{2,14},{4,0},{6,2},{9,5},{11,7},{13,9},{15,11},{16,28},{18,... | collective-permute-start | bytes 196616 | tf_op jit(solution)/shard_map/return_y/ppermute | solution.py:36
  (123 shorter events, 35.4 us)
Async XLA Ops:
  12.0 8.4 %collective-permute-start = (bf16[1056,128]{1,0:T(8,128)(2,1)S(1)}, bf16[1056,128]{1,0:T(8,128)(2,1)S(1)}, u32[]{:S(2)}, u32[]{:S(2)}) collective-permute-start(bf16[1056,128]{1,0:T(8,128)(2,1)S(1)} %get-tuple-element.41), channel_id=1, source_target_pairs={{1,13},{3,15},{4,0},{6,2},{8,4},{10,6},{13,9},{15,11},{17,29},{19,... | collective-permute-start | bytes 811016 | tf_op jit(solution)/shard_map/gather_y/ppermute | solution.py:36
  15.5 9.9 %collective-permute-start.1 = (bf16[1056,128]{1,0:T(8,128)(2,1)S(1)}, bf16[1056,128]{1,0:T(8,128)(2,1)S(1)}, u32[]{:S(2)}, u32[]{:S(2)}) collective-permute-start(bf16[1056,128]{1,0:T(8,128)(2,1)S(1)} %get-tuple-element.40), channel_id=1, source_target_pairs={{1,9},{3,11},{5,13},{7,15},{8,0},{10,2},{12,4},{14,6},{17,25},{19,... | collective-permute-start | bytes 811016 | tf_op jit(solution)/shard_map/gather_y/ppermute | solution.py:36
  16.8 8.8 %collective-permute-start.2 = (bf16[1056,128]{1,0:T(8,128)(2,1)S(1)}, bf16[1056,128]{1,0:T(8,128)(2,1)S(1)}, u32[]{:S(2)}, u32[]{:S(2)}) collective-permute-start(bf16[1056,128]{1,0:T(8,128)(2,1)S(1)} %get-tuple-element.41), channel_id=1, source_target_pairs={{0,4},{2,6},{5,9},{7,11},{9,13},{11,15},{12,0},{14,2},{16,20},{18,... | collective-permute-start | bytes 811016 | tf_op jit(solution)/shard_map/gather_y/ppermute | solution.py:36
  26.8 15.0 %collective-permute-start.3 = (bf16[4224,128]{1,0:T(8,128)(2,1)S(1)}, bf16[4224,128]{1,0:T(8,128)(2,1)S(1)}, u32[]{:S(2)}, u32[]{:S(2)}) collective-permute-start(bf16[4224,128]{1,0:T(8,128)(2,1)S(1)} %pad_maximum_fusion), channel_id=1, source_target_pairs={{0,1},{2,3},{4,5},{6,7},{9,8},{11,10},{13,12},{15,14},{16,17},{18,... | collective-permute-start | bytes 3244040 | tf_op jit(solution)/shard_map/gather_z/ppermute | solution.py:36
  29.1 17.2 %collective-permute-start.4 = (bf16[1088,128]{1,0:T(8,128)(2,1)S(1)}, bf16[1088,128]{1,0:T(8,128)(2,1)S(1)}, u32[]{:S(2)}, u32[]{:S(2)}) collective-permute-start(bf16[1088,128]{1,0:T(8,128)(2,1)S(1)} %pad_maximum_fusion.3), channel_id=1, source_target_pairs={{0,16},{2,18},{4,20},{6,22},{9,24},{11,26},{13,28},{15,30},{16,32}... | collective-permute-start | bytes 835592 | tf_op jit(solution)/shard_map/gather_z/ppermute | solution.py:36
  32.4 13.8 %collective-permute-start.5 = (bf16[2112,128]{1,0:T(8,128)(2,1)S(1)}, bf16[2112,128]{1,0:T(8,128)(2,1)S(1)}, u32[]{:S(2)}, u32[]{:S(2)}) collective-permute-start(bf16[2112,128]{1,0:T(8,128)(2,1)S(1)} %get-tuple-element.26), channel_id=1, source_target_pairs={{0,241},{2,243},{4,245},{6,247},{9,249},{11,251},{13,253},{15,255}... | collective-permute-start | bytes 1622024 | tf_op jit(solution)/shard_map/gather_z/ppermute | solution.py:36
  38.0 8.2 %collective-permute-start.6 = (bf16[512,128]{1,0:T(8,128)(2,1)S(1)}, bf16[512,128]{1,0:T(8,128)(2,1)S(1)}, u32[]{:S(2)}, u32[]{:S(2)}) collective-permute-start(bf16[512,128]{1,0:T(8,128)(2,1)S(1)} %get-tuple-element.25), channel_id=1, source_target_pairs={{0,240},{2,242},{4,244},{6,246},{9,248},{11,250},{13,252},{15,254}... | collective-permute-start | bytes 393224 | tf_op jit(solution)/shard_map/gather_z/ppermute | solution.py:36
  76.0 16.3 %collective-permute-start.11 = (bf16[1536,128]{1,0:T(8,128)(2,1)}, bf16[1536,128]{1,0:T(8,128)(2,1)S(1)}, u32[]{:S(2)}, u32[]{:S(2)}) collective-permute-start(bf16[1536,128]{1,0:T(8,128)(2,1)} %get-tuple-element.18), channel_id=1, source_target_pairs={{1,0},{3,2},{5,4},{7,6},{8,9},{10,11},{12,13},{14,15},{17,16},{19,... | collective-permute-start | bytes 1179656 | tf_op jit(solution)/shard_map/return_z/ppermute | solution.py:36
  77.6 16.4 %collective-permute-start.15 = (bf16[512,512]{1,0:T(8,128)(2,1)S(1)}, bf16[512,512]{1,0:T(8,128)(2,1)S(1)}, u32[]{:S(2)}, u32[]{:S(2)}) collective-permute-start(bf16[512,512]{1,0:T(8,128)(2,1)S(1)} %all_gather.3), channel_id=1, source_target_pairs={{1,241},{3,243},{17,1},{19,3},{33,17},{35,19},{49,33},{51,35},{65,... | collective-permute-start | bytes 1572872 | tf_op jit(solution)/shard_map/spread_grad/ppermute | solution.py:36
  78.3 18.1 %collective-permute-start.17 = (bf16[512,512]{1,0:T(8,128)(2,1)S(1)}, bf16[512,512]{1,0:T(8,128)(2,1)S(1)}, u32[]{:S(2)}, u32[]{:S(2)}) collective-permute-start(bf16[512,512]{1,0:T(8,128)(2,1)S(1)} %all_gather.3), channel_id=1, source_target_pairs={{0,8},{1,249},{2,10},{3,251},{4,12},{6,14},{8,0},{9,1},{10,2},{11,... | collective-permute-start | bytes 1572872 | tf_op jit(solution)/shard_map/spread_grad/ppermute | solution.py:36
  83.0 21.2 %collective-permute-start.18 = (bf16[512,512]{1,0:T(8,128)(2,1)S(1)}, bf16[512,512]{1,0:T(8,128)(2,1)S(1)}, u32[]{:S(2)}, u32[]{:S(2)}) collective-permute-start(bf16[512,512]{1,0:T(8,128)(2,1)S(1)} %all_gather.3), channel_id=1, source_target_pairs={{0,12},{1,253},{2,14},{3,255},{4,0},{6,2},{8,4},{9,5},{10,6},{11,7... | collective-permute-start | bytes 1572872 | tf_op jit(solution)/shard_map/spread_grad/ppermute | solution.py:36
  87.2 22.1 %collective-permute-start.16 = (bf16[512,512]{1,0:T(8,128)(2,1)S(1)}, bf16[512,512]{1,0:T(8,128)(2,1)S(1)}, u32[]{:S(2)}, u32[]{:S(2)}) collective-permute-start(bf16[512,512]{1,0:T(8,128)(2,1)S(1)} %all_gather.3), channel_id=1, source_target_pairs={{0,4},{1,245},{2,6},{3,247},{4,8},{6,10},{8,12},{9,13},{10,14},{11... | collective-permute-start | bytes 1572872 | tf_op jit(solution)/shard_map/spread_grad/ppermute | solution.py:36
  92.3 17.5 %collective-permute-start.8 = (bf16[2048,128]{1,0:T(8,128)(2,1)S(1)}, bf16[2048,128]{1,0:T(8,128)(2,1)S(1)}, u32[]{:S(2)}, u32[]{:S(2)}) collective-permute-start(bf16[2048,128]{1,0:T(8,128)(2,1)S(1)} %copy-done.8), channel_id=1, source_target_pairs={{1,16},{3,18},{5,20},{7,22},{9,25},{11,27},{13,29},{15,31},{17,32}... | collective-permute-start | bytes 1572872 | tf_op jit(solution)/shard_map/return_z/ppermute | solution.py:36
  93.9 15.9 %collective-permute-start.9 = (bf16[512,128]{1,0:T(8,128)(2,1)S(1)}, bf16[512,128]{1,0:T(8,128)(2,1)S(1)}, u32[]{:S(2)}, u32[]{:S(2)}) collective-permute-start(bf16[512,128]{1,0:T(8,128)(2,1)S(1)} %slice.122), channel_id=1, source_target_pairs={{0,16},{2,18},{4,20},{6,22},{8,25},{10,27},{12,29},{14,31},{16,32}... | collective-permute-start | bytes 393224 | tf_op jit(solution)/shard_map/return_z/ppermute | solution.py:36
  96.3 13.7 %collective-permute-start.10 = (bf16[1024,128]{1,0:T(8,128)(2,1)S(1)}, bf16[1024,128]{1,0:T(8,128)(2,1)S(1)}, u32[]{:S(2)}, u32[]{:S(2)}) collective-permute-start(bf16[1024,128]{1,0:T(8,128)(2,1)S(1)} %slice.124), channel_id=1, source_target_pairs={{0,240},{2,242},{4,244},{6,246},{8,249},{10,251},{12,253},{14,255}... | collective-permute-start | bytes 786440 | tf_op jit(solution)/shard_map/return_z/ppermute | solution.py:36
  111.9 7.5 %collective-permute-start.21 = (bf16[64,512]{1,0:T(8,128)(2,1)S(1)}, bf16[64,512]{1,0:T(8,128)(2,1)S(1)}, u32[]{:S(2)}, u32[]{:S(2)}) collective-permute-start(bf16[64,512]{1,0:T(8,128)(2,1)S(1)} %add_convert_fusion.2), channel_id=1, source_target_pairs={{0,32},{1,33},{2,34},{3,35},{4,36},{5,37},{6,38},{7,39},{8,40},{9,... | collective-permute-start | bytes 196616 | tf_op jit(solution)/shard_map/reduce_w/ppermute | solution.py:36
  121.5 12.8 %collective-permute-start.23 = (bf16[64,512]{1,0:T(8,128)(2,1)S(1)}, bf16[64,512]{1,0:T(8,128)(2,1)S(1)}, u32[]{:S(2)}, u32[]{:S(2)}) collective-permute-start(bf16[64,512]{1,0:T(8,128)(2,1)S(1)} %add_convert_fusion.1), channel_id=1, source_target_pairs={{0,64},{1,65},{2,66},{3,67},{4,68},{5,69},{6,70},{7,71},{8,72},{9,... | collective-permute-start | bytes 196616 | tf_op jit(solution)/shard_map/reduce_w/ppermute | solution.py:36
  125.8 11.1 %collective-permute-start.24 = (bf16[64,512]{1,0:T(8,128)(2,1)S(1)}, bf16[64,512]{1,0:T(8,128)(2,1)S(1)}, u32[]{:S(2)}, u32[]{:S(2)}) collective-permute-start(bf16[64,512]{1,0:T(8,128)(2,1)S(1)} %add_convert_fusion.1), channel_id=1, source_target_pairs={{0,128},{1,129},{2,130},{3,131},{4,132},{5,133},{6,134},{7,135},{8... | collective-permute-start | bytes 196616 | tf_op jit(solution)/shard_map/reduce_w/ppermute | solution.py:36
  128.5 10.7 %collective-permute-start.25 = (bf16[64,512]{1,0:T(8,128)(2,1)S(1)}, bf16[64,512]{1,0:T(8,128)(2,1)S(1)}, u32[]{:S(2)}, u32[]{:S(2)}) collective-permute-start(bf16[64,512]{1,0:T(8,128)(2,1)S(1)} %add_convert_fusion.1), channel_id=1, source_target_pairs={{0,192},{1,193},{2,194},{3,195},{4,196},{5,197},{6,198},{7,199},{8... | collective-permute-start | bytes 196616 | tf_op jit(solution)/shard_map/reduce_w/ppermute | solution.py:36
  130.5 11.9 %collective-permute-start.14 = (bf16[1024,128]{1,0:T(8,128)(2,1)S(1)}, bf16[1024,128]{1,0:T(8,128)(2,1)S(1)}, u32[]{:S(2)}, u32[]{:S(2)}) collective-permute-start(bf16[1024,128]{1,0:T(8,128)(2,1)S(1)} %get-tuple-element.35), channel_id=1, source_target_pairs={{0,12},{2,14},{4,0},{6,2},{9,5},{11,7},{13,9},{15,11},{16,28},{18,... | collective-permute-start | bytes 786440 | tf_op jit(solution)/shard_map/return_y/ppermute | solution.py:36
  132.3 14.1 %collective-permute-start.12 = (bf16[1024,128]{1,0:T(8,128)(2,1)S(1)}, bf16[1024,128]{1,0:T(8,128)(2,1)S(1)}, u32[]{:S(2)}, u32[]{:S(2)}) collective-permute-start(bf16[1024,128]{1,0:T(8,128)(2,1)S(1)} %get-tuple-element.33), channel_id=1, source_target_pairs={{0,4},{2,6},{4,8},{6,10},{9,13},{11,15},{13,1},{15,3},{16,20},{18,... | collective-permute-start | bytes 786440 | tf_op jit(solution)/shard_map/return_y/ppermute | solution.py:36
  134.3 12.2 %collective-permute-start.13 = (bf16[1024,128]{1,0:T(8,128)(2,1)S(1)}, bf16[1024,128]{1,0:T(8,128)(2,1)S(1)}, u32[]{:S(2)}, u32[]{:S(2)}) collective-permute-start(bf16[1024,128]{1,0:T(8,128)(2,1)S(1)} %get-tuple-element.34), channel_id=1, source_target_pairs={{0,8},{2,10},{4,12},{6,14},{9,1},{11,3},{13,5},{15,7},{16,24},{18,... | collective-permute-start | bytes 786440 | tf_op jit(solution)/shard_map/return_y/ppermute | solution.py:36
  139.2 9.9 %collective-permute-start.26 = (bf16[64,512]{1,0:T(8,128)(2,1)S(1)}, bf16[64,512]{1,0:T(8,128)(2,1)S(1)}, u32[]{:S(2)}, u32[]{:S(2)}) collective-permute-start(bf16[64,512]{1,0:T(8,128)(2,1)S(1)} %add_convert_fusion), channel_id=1, source_target_pairs={{0,4},{2,6},{4,8},{6,10},{9,13},{11,15},{13,1},{15,3},{16,20},{18,... | collective-permute-start | bytes 196616 | tf_op jit(solution)/shard_map/return_y/ppermute | solution.py:36
  141.2 8.0 %collective-permute-start.27 = (bf16[64,512]{1,0:T(8,128)(2,1)S(1)}, bf16[64,512]{1,0:T(8,128)(2,1)S(1)}, u32[]{:S(2)}, u32[]{:S(2)}) collective-permute-start(bf16[64,512]{1,0:T(8,128)(2,1)S(1)} %add_convert_fusion), channel_id=1, source_target_pairs={{0,8},{2,10},{4,12},{6,14},{9,1},{11,3},{13,5},{15,7},{16,24},{18,... | collective-permute-start | bytes 196616 | tf_op jit(solution)/shard_map/return_y/ppermute | solution.py:36
  (20 other events, 120.0 us)

commit v2 on v0

v2 whole, which is shorter than its diff:
```python
import jax
import jax.numpy as jnp
from jax import lax
from jax.experimental import pallas as pl
from jax.experimental.pallas import tpu as pltpu
from jax.sharding import PartitionSpec as P

HD = 64
BLK = 512
HALF = BLK // 2
WIN = 6 * BLK
TILE = 256
META = 32
UNIT = BLK + META
FULL = UNIT + HALF
F32 = jnp.float32
BF16 = jnp.bfloat16
ABSENT = -1e30


def send(block, target):
    blocks = lax.axis_size("blk")
    route = [(i, target(i) % blocks) for i in range(blocks) if target(i) is not None]
    return lax.ppermute(block, "blk", route)


def swap(block, mask):
    return send(block, lambda i: i ^ mask)


def contract(a, b, dim_a, dim_b):
    return lax.dot_general(
        a, b, (((dim_a,), (dim_b,)), ((), ())), preferred_element_type=F32
    )


def lanes(rows):
    return lax.broadcasted_iota(jnp.int32, (rows, 2 * HD), 1)


def units_kernel(place_ref, near_ref, slots_ref, keys_ref, values_ref, queries_ref, own, theirs):
    place = place_ref[0]
    blocks = place_ref[1]
    slots = slots_ref[...] - place * BLK
    slots = jnp.where(slots < 0, slots + blocks * BLK, slots)
    high = lax.broadcasted_iota(jnp.int32, (16, 2 * BLK), 0)
    low = lax.broadcasted_iota(jnp.int32, (128, 2 * BLK), 0)
    row_hit = (high == lax.shift_right_logical(slots, 7)).astype(F32).astype(BF16)
    lane_hit = (low == (slots & 127)).astype(F32).astype(BF16)
    count = contract(row_hit, lane_hit, 1, 1)[0:8, :]
    coarse = jnp.floor(count * (1.0 / 32.0))

    def offset(j):
        hop = near_ref[0, j] - place
        hop = jnp.where(hop < -2, hop + blocks, hop)
        return jnp.where(hop > 2, hop - blocks, hop).astype(F32)

    lane = lanes(16)
    near = jnp.where(lane == 0, offset(0), jnp.where(lane == 1, offset(1), 0.0))
    meta = jnp.concatenate([coarse, count - coarse * 32.0, near]).astype(BF16)

    def rolled(rows):
        return pltpu.roll(rows.astype(F32), HD, 1).astype(BF16)

    keys = keys_ref[...]
    values = values_ref[...]
    top = queries_ref[0:HALF, :]
    end = queries_ref[HALF:BLK, :]
    left = lanes(BLK) < HD
    short = lanes(HALF) < HD

    def put(out, j):
        if j == 0:
            out[0:BLK, :] = jnp.where(left, keys, rolled(values))
            out[UNIT:FULL, :] = jnp.where(short, top, rolled(end))
        else:
            out[0:BLK, :] = jnp.where(left, rolled(keys), values)
            out[UNIT:FULL, :] = jnp.where(short, rolled(top), end)
        out[BLK:UNIT, :] = meta

    @pl.when(lax.rem(place, 2) == 0)
    def _():
        put(own, 0)
        put(theirs, 1)

    @pl.when(lax.rem(place, 2) == 1)
    def _():
        put(own, 1)
        put(theirs, 0)


def make_units(*operands):
    smem = pl.BlockSpec(memory_space=pltpu.SMEM)
    vmem = pl.BlockSpec(memory_space=pltpu.VMEM)
    unit = jax.ShapeDtypeStruct((FULL, 2 * HD), BF16)
    return pl.pallas_call(
        units_kernel,
        out_shape=(unit, unit),
        in_specs=[smem, smem] + [vmem] * 4,
        out_specs=(vmem, vmem),
        name="units",
    )(*operands)


def forward_prepare(
    member, own_ref, mate_ref, left_ref, right_ref, last_ref, kv, query, meta, bias, weight
):
    def put_keys(slot, rows):
        kv[pl.ds(pl.multiple_of(slot * BLK, BLK), BLK), :] = rows

    def put_meta(slot, rows):
        meta[pl.ds(pl.multiple_of(slot * META, META), META), :] = rows

    for near, far in ((own_ref, 0), (mate_ref, 1)):
        at = member if far == 0 else 1 - member
        put_keys(2 + at, near[0:BLK, :])
        put_meta(2 + at, near[BLK:UNIT, :])
        for first, pair in ((0, left_ref), (4, right_ref)):
            base = far * UNIT
            put_keys(first + at, pair[base : base + BLK, :])
            put_meta(first + at, pair[base + BLK : base + UNIT, :])
    put_keys(6, last_ref[...])

    def put_query(slot, rows):
        scaled = rows * 0.125
        zero = jnp.zeros_like(scaled)
        at = pl.multiple_of(slot * BLK, BLK)
        low = lanes(HALF) < HD
        flipped = pltpu.roll(scaled.astype(F32), HD, 1).astype(BF16)
        query[pl.ds(at, HALF), :] = jnp.where(low, scaled, zero)
        query[pl.ds(at + HALF, HALF), :] = jnp.where(low, flipped, zero)

    put_query(member, own_ref[UNIT:FULL, :])
    put_query(1 - member, mate_ref[UNIT:FULL, :])
    put_query(2, right_ref[2 * UNIT : 2 * UNIT + HALF, :])

    def counts(patch):
        rows = meta[patch * META : (patch + 1) * META, :].astype(F32)
        return rows[0:8, :] * 32.0 + rows[8:16, :]

    eye = lax.broadcasted_iota(jnp.int32, (128, 128), 0) == lax.broadcasted_iota(
        jnp.int32, (128, 128), 1
    )
    for job in range(2):
        near = meta[(2 + job) * META + 16 : (2 + job) * META + 32, :].astype(F32)[0:1, :]

        def chosen(patch, near=near, job=job):
            if patch < 0 or patch > 5:
                return None
            if patch == 2 + job:
                return jnp.ones((1, 1), F32)
            offset = float(patch - 2 - job)
            hit = (near[:, 0:1] == offset) | (near[:, 1:2] == offset)
            return hit.astype(F32)

        for block in range(6):
            slot = block + job
            total = jnp.zeros((4, 128), F32)
            if abs(slot - 2 - job) <= 2 and slot <= 5:
                total = total + counts(slot)[0:4, :] * chosen(slot)
            if abs(slot - 3 - job) <= 2 and slot >= 1:
                total = total + counts(slot - 1)[4:8, :] * chosen(slot - 1)
            logs = jnp.where(total > 0.5, jnp.log(jnp.maximum(total, 1.0)), ABSENT)
            for row in range(4):
                at = block * BLK + row * 128
                bias[job, 0:1, at : at + 128] = logs[row : row + 1, :]
        own = counts(2 + job)
        for row in range(8):
            spread = jnp.where(eye, jnp.broadcast_to(own[row : row + 1, :], (128, 128)), 0.0)
            weight[job, row * 128 : (row + 1) * 128, :] = jnp.sum(spread, axis=1, keepdims=True)


def attention_kernel(
    member_ref, own_ref, mate_ref, left_ref, right_ref, last_ref, cot_own, cot_mate, cot_rim,
    left_out, right_out, last_out, pair_out, mine_out, mate_out, rim_out,
    kv, query, cot, meta, bias, weight, kv_acc, row_acc,
):
    member = member_ref[0]
    forward_prepare(
        member, own_ref, mate_ref, left_ref, right_ref, last_ref, kv, query, meta, bias, weight
    )

    def put(slot, rows):
        zero = jnp.zeros_like(rows)
        at = pl.multiple_of(slot * BLK, BLK)
        high = lanes(HALF) >= HD
        flipped = pltpu.roll(rows.astype(F32), HD, 1).astype(BF16)
        cot[pl.ds(at, HALF), :] = jnp.where(high, flipped, zero)
        cot[pl.ds(at + HALF, HALF), :] = jnp.where(high, rows, zero)

    put(member, cot_own[...])
    put(1 - member, cot_mate[...])
    put(2, cot_rim[...])
    kv_acc[...] = jnp.zeros_like(kv_acc)
    row_acc[...] = jnp.zeros_like(row_acc)

    def step(tile, carry):
        keys = [kv[job * BLK : job * BLK + WIN, :] for job in range(2)]
        rows = [pl.ds(pl.multiple_of(job * BLK + tile * TILE, TILE), TILE) for job in range(2)]
        q = [query[at, :] for at in rows]
        d = [cot[at, :] for at in rows]
        at = pl.ds(pl.multiple_of(tile * TILE, TILE), TILE)
        times = [weight[job, at, :] for job in range(2)]

        def softmax(job):
            peak = jnp.max(scores[job], axis=1, keepdims=True)
            grown = jnp.exp(scores[job] - peak)
            probs = grown * (times[job] / jnp.sum(grown, axis=1, keepdims=True))
            return probs, probs.astype(BF16)

        def score_grads(job, probs, attn, d_probs):
            delta = jnp.sum(attn * d[job].astype(F32), axis=1, keepdims=True)
            delta = delta / jnp.maximum(times[job], 1.0)
            return (probs * (d_probs - delta)).astype(BF16)

        def gather_grads(job, low, attn, d_scores):
            d_query = contract(d_scores, keys[job], 1, 0) * 0.125
            row_acc[rows[job], :] += jnp.where(lanes(TILE) < HD, d_query, attn)
            first = job * BLK
            kv_acc[:, first : first + WIN] += contract(q[job], d_scores, 0, 0) + contract(
                d[job], low, 0, 0
            )

        scores = [contract(q[job], keys[job], 1, 1) + bias[job] for job in range(2)]
        probs_a, low_a = softmax(0)
        d_probs_a = contract(d[0], keys[0], 1, 1)
        attn_a = contract(low_a, keys[0], 1, 0)
        probs_b, low_b = softmax(1)
        d_scores_a = score_grads(0, probs_a, attn_a, d_probs_a)
        d_probs_b = contract(d[1], keys[1], 1, 1)
        attn_b = contract(low_b, keys[1], 1, 0)
        gather_grads(0, low_a, attn_a, d_scores_a)
        d_scores_b = score_grads(1, probs_b, attn_b, d_probs_b)
        gather_grads(1, low_b, attn_b, d_scores_b)
        return carry

    lax.fori_loop(0, 2 * BLK // TILE, step, 0)

    def grads(slot):
        return kv_acc[:, slot * BLK : (slot + 1) * BLK].T

    def packed_rows(slot):
        top = row_acc[slot * BLK : slot * BLK + HALF, :]
        low = row_acc[slot * BLK + HALF : (slot + 1) * BLK, :]
        return jnp.where(lanes(HALF) < HD, top, pltpu.roll(low, HD, 1))

    def packed_attn(slot):
        at = pl.multiple_of(slot * BLK, BLK)
        top = row_acc[pl.ds(at, HALF), :]
        low = row_acc[pl.ds(at + HALF, HALF), :]
        return jnp.where(lanes(HALF) < HD, pltpu.roll(top, HD, 1), low).astype(BF16)

    for block in range(2):
        at = slice(block * BLK, (block + 1) * BLK)
        left_out[at, :] = grads(block).astype(BF16)
        right_out[at, :] = grads(4 + block).astype(BF16)
        pair_out[block, 0:BLK, :] = grads(2 + block)
        pair_out[block, BLK : BLK + HALF, :] = packed_rows(block)
    right_out[2 * BLK : 2 * BLK + HALF, :] = packed_rows(2).astype(BF16)
    last_out[...] = grads(6).astype(BF16)
    mine_out[...] = packed_attn(member)
    mate_out[...] = packed_attn(1 - member)
    rim_out[...] = packed_attn(2)


def attention(*operands):
    vmem = pl.BlockSpec(memory_space=pltpu.VMEM)
    return pl.pallas_call(
        attention_kernel,
        out_shape=(
            jax.ShapeDtypeStruct((2 * BLK, 2 * HD), BF16),
            jax.ShapeDtypeStruct((2 * BLK + HALF, 2 * HD), BF16),
            jax.ShapeDtypeStruct((BLK, 2 * HD), BF16),
            jax.ShapeDtypeStruct((2, BLK + HALF, 2 * HD), F32),
            *[jax.ShapeDtypeStruct((HALF, 2 * HD), BF16)] * 3,
        ),
        in_specs=[pl.BlockSpec(memory_space=pltpu.SMEM)] + [vmem] * 8,
        out_specs=(vmem,) * 7,
        scratch_shapes=[
            pltpu.VMEM((7 * BLK, 2 * HD), BF16),
            pltpu.VMEM((3 * BLK, 2 * HD), BF16),
            pltpu.VMEM((3 * BLK, 2 * HD), BF16),
            pltpu.VMEM((6 * META, 2 * HD), BF16),
            pltpu.VMEM((2, 1, WIN), F32),
            pltpu.VMEM((2, 2 * BLK, 1), F32),
            pltpu.VMEM((2 * HD, 7 * BLK), F32),
            pltpu.VMEM((3 * BLK, 2 * HD), F32),
        ],
        compiler_params=pltpu.CompilerParams(vmem_limit_bytes=56 * 1024 * 1024),
        cost_estimate=pl.CostEstimate(
            flops=20_000_000_000, bytes_accessed=4_000_000, transcendentals=6_300_000
        ),
        name="attention_backward",
    )(*operands)


def local(queries, keys, values, out_grad, w_out, slot_point, neighbours):
    place = lax.axis_index("blk")
    blocks = lax.axis_size("blk")
    member = lax.rem(place, 2)
    second = member == 1
    flag = jnp.reshape(member, (1,)).astype(jnp.int32)

    def pick(if_first, if_second):
        return jnp.where(second, if_second, if_first)

    def folded(rows):
        return jnp.concatenate([rows[:HALF], rows[HALF:]], axis=1)

    def of_head(array, j):
        return array[:, j * HD : (j + 1) * HD]

    with jax.named_scope("units"):
        where = jnp.stack([place, jnp.full_like(place, blocks)]).astype(jnp.int32)
        own, theirs = make_units(where, neighbours, slot_point, keys, values, queries)

    with jax.named_scope("gather_keys"):
        mate = swap(theirs, 1)
        rim_query = pick(own[UNIT:], mate[UNIT:])
        pair = jnp.concatenate([own[:UNIT], mate[:UNIT], rim_query])
        left = send(pair[: 2 * UNIT], lambda i: i + 2)
        right = send(pair, lambda i: i - 2)
        last = send(pick(own[:BLK], mate[:BLK]), lambda i: i - 4)

    with jax.named_scope("cotangent"):
        head = lax.axis_index("head")
        got = [out_grad] + [
            lax.ppermute(out_grad, "head", [(i, i ^ k) for i in range(4)]) for k in (1, 2, 3)
        ]
        odd = lax.rem(head, 2) == 1
        got = [jnp.where(odd, got[k ^ 1], got[k]) for k in range(4)]
        upper = head >= 2
        grad_all = jnp.concatenate(
            [jnp.where(upper, got[k ^ 2], got[k]) for k in range(4)], axis=1
        )
        d_attn = jnp.dot(grad_all, w_out.T, preferred_element_type=F32).astype(BF16)
        cots = [folded(of_head(d_attn, j)) for j in range(2)]
        cot_own = pick(cots[0], cots[1])
        cot_mate = swap(pick(cots[1], cots[0]), 1)
        cot_rim = send(pick(cot_own, cot_mate), lambda i: i - 2)

    with jax.named_scope("attention"):
        left, right, last, cot_rim, grad_sent = lax.optimization_barrier(
            (left, right, last, cot_rim, grad_all)
        )
        grad_mate = swap(grad_sent, 1)
        left_grad, right_grad, last_grad, pair_grad, mine, theirs, rim = attention(
            flag, own, mate, left, right, last, cot_own, cot_mate, cot_rim
        )
        left_grad, right_grad, last_grad, pair_grad, mine, theirs, rim, grad_mate = (
            lax.optimization_barrier(
                (left_grad, right_grad, last_grad, pair_grad, mine, theirs, rim, grad_mate)
            )
        )

    half = blocks // 2
    planes = [
        [up * half + z * 4 + y for z in range(half // 4)] for up in range(2) for y in range(4)
    ]
    others = [
        [up * half + z * 4 + y for up in range(2) for y in range(4)] for z in range(half // 4)
    ]

    def exchange(rows, groups):
        return lax.all_to_all(rows, "blk", 0, 0, axis_index_groups=groups, tiled=True)

    def copies(rows):
        return jnp.broadcast_to(rows[None], (8,) + rows.shape).reshape(-1, rows.shape[1])

    with jax.named_scope("return_attention"):
        rim_got = send(rim, lambda i: i + 2)
        from_left = send(right_grad, lambda i: i + 2)
        from_right = send(left_grad, lambda i: i - 2)
        from_last = send(last_grad, lambda i: i + 4)

        def plus_rim(rows):
            return (rows.astype(F32) + rim_got.astype(F32)).astype(BF16)

        mine = pick(plus_rim(mine), mine)
        theirs = pick(theirs, plus_rim(theirs))

    with jax.named_scope("w_out_grad"):

        def part(attn, grad, half):
            return lax.dot_general(
                attn[:, half * HD : (half + 1) * HD],
                grad[half * HALF : (half + 1) * HALF],
                (((0,), (0,)), ((), ())),
                preferred_element_type=F32,
            )

        w_part = part(mine, grad_all, 0) + part(mine, grad_all, 1)
        w_part = w_part + part(theirs, grad_mate, 0) + part(theirs, grad_mate, 1)
        around = exchange(w_part, planes)
        around, from_left, from_right, from_last = lax.optimization_barrier(
            (around, from_left, from_right, from_last)
        )

    with jax.named_scope("totals"):
        from_left = from_left.astype(F32)
        from_right = from_right.astype(F32)
        first = pair_grad[0] + jnp.concatenate(
            [from_left[:BLK] + from_right[:BLK] + from_last.astype(F32), from_left[2 * BLK :]]
        )
        other = pair_grad[1] + jnp.concatenate(
            [from_left[BLK : 2 * BLK] + from_right[BLK:], jnp.zeros((HALF, 2 * HD), F32)]
        )
        mine = pick(first, other)
        got = swap(pick(other, first).astype(BF16), 1)
        width = around.shape[1]
        around = jnp.sum(around.reshape(8, HD // 8, width), axis=0)
        around = exchange(copies(around), others)
        around = jnp.sum(around.reshape(4, HD // 4, width), axis=0).astype(BF16)
        around, got = lax.optimization_barrier((around, got))
        around = exchange(copies(around), planes)
        around = jnp.swapaxes(around.reshape(8, 2, HD // 8, width), 0, 1)
        w_grad = around.reshape(2 * HD, width).astype(F32)
        heads = [pick(mine, got.astype(F32)), pick(got.astype(F32), mine)]
        d_key = jnp.concatenate([u[:BLK, :HD] for u in heads], axis=1).astype(BF16)
        d_value = jnp.concatenate([u[:BLK, HD:] for u in heads], axis=1).astype(BF16)
        d_query = jnp.concatenate(
            [jnp.concatenate([u[BLK:, :HD], u[BLK:, HD:]], axis=0) for u in heads], axis=1
        ).astype(BF16)
    return d_query, d_key, d_value, w_grad


def solution(mesh):
    placed = (
        P("blk", "head"),
        P("blk", "head"),
        P("blk", "head"),
        P("blk", "head"),
        P("head", None),
        P("blk", None),
        P("blk", None),
    )
    return jax.shard_map(
        local,
        mesh=mesh,
        in_specs=placed,
        out_specs=(P("blk", "head"), P("blk", "head"), P("blk", "head"), P("head", None)),
        check_vma=False,
    )
```

time: 894 us -> 123 us (0.14); the launches traced: 883 us -> 123 us
  waiting for transfers between devices: 610 us -> 32.2 us
  other arithmetic: 76.9 us -> 4.62 us
  matrix products: 53.2 us -> 1.82 us
  local copies, waits for them, and re-layouts: 40.5 us -> 5.53 us
  starting transfers between devices: 83.8 us -> 50.2 us
  Pallas kernels: 0 us -> 27.2 us
  between operations: 18.8 us -> 0.92 us
    psum x1 -> x0, waiting for transfers between devices: 588 us -> none  [local(): weight_grad = lax.psum(weight_acc, 'blk')]
    dot_general x14 -> x5, matrix products: 53.2 us -> 1.82 us  [the longest x4 1.54 us: part(): lax.dot_general(attn[:, half * HD:(half + 1) * HD], grad[half * HALF:(hal...]
    ppermute x27 -> x15, starting transfers between devices: 83.7 us -> 34.6 us  [the longest x12 32.4 us: send(): return lax.ppermute(block, 'blk', route)]
    scatter-add x3 -> x0, other arithmetic: 43.3 us -> none  [the longest x1 18.5 us: local(): value_acc = value_acc.at[key_loc].add(jnp.concatenate(dv_all, axis=1))]
    pallas_call x0 -> x2, Pallas kernels: none -> 27.2 us  [the longest x1 25 us: attention(): pl.pallas_call(attention_kernel, out_shape=(jax.ShapeDtypeStruct((2 * BLK...]
    gather x4 -> x0, local copies, waits for them, and re-layouts: 26.9 us -> none  [the longest x1 9.16 us: local(): k_rows = key_win[key_loc]]
    convert_element_type x5 -> x4, other arithmetic: 17 us -> 0.17 us  [the longest x1 0.07 us: local(): got = swap(pick(other, first).astype(BF16), 1)]
    all_to_all x0 -> x3, starting transfers between devices: none -> 15.6 us  [exchange(): lax.all_to_all(rows, 'blk', 0, 0, axis_index_groups=groups, tiled=True)]
  transfers between devices with their start and end apart: 29 -> 18, of which waited for: 7 -> 8; matrix products, arithmetic and copies ran while one was open for 6% -> 6% of each run, Pallas kernels for 0% -> 22%
where the time goes in v2:
time: 123 us
  starting transfers between devices  50.2 us (41%)
  waiting for transfers between devices  32.2 us (26%)
  Pallas kernels  27.2 us (22%)
  local copies, waits for them, and re-layouts  5.53 us (4%)
  other arithmetic  4.62 us (4%)
  matrix products  1.82 us (1%)
    ppermute x12, starting transfers between devices, send(): return lax.ppermute(block, 'blk', route)  32.4 us
    pallas_call x1, Pallas kernels, attention(): pl.pallas_call(attention_kernel, out_shape=(jax.ShapeDtypeStruct((2 * BLK...  25 us
    ppermute x12, waiting for transfers between devices, send(): return lax.ppermute(block, 'blk', route)  19.2 us
    all_to_all x3, starting transfers between devices, exchange(): lax.all_to_all(rows, 'blk', 0, 0, axis_index_groups=groups, tiled=True)  15.6 us
    all_to_all x3, waiting for transfers between devices, exchange(): lax.all_to_all(rows, 'blk', 0, 0, axis_index_groups=groups, tiled=True)  13 us
  transfers between devices with their start and end apart: 18, of which 8 were waited for; matrix products, arithmetic and copies ran while one was open for 6% of the time, Pallas kernels for 22%

profile of v2, /device:TPU:8, one launch (start us, length us, event | category | flops | bytes accessed | tf_op | source)
XLA Modules:
  0.0 122.5 jit_solution(2869362408511614162)
XLA Ops:
  0.6 1.6 %collective-permute-start.5 = (bf16[512,128]{1,0:T(8,128)(2,1)}, bf16[512,128]{1,0:T(8,128)(2,1)S(1)}, u32[]{:S(2)}, u32[]{:S(2)}) collective-permute-start(bf16[512,128]{1,0:T(8,128)(2,1)} %param.10), channel_id=1, source_target_pairs={{0,2},{1,3},{2,0},{3,1},{4,6},{5,7},{6,4},{7,5},{8,10},{9,11},{10,... | collective-permute-start | bytes 393224 | tf_op jit(solution)/shard_map/cotangent/ppermute | solution.py:328
  3.5 2.2 %units.1 = (bf16[800,128]{1,0:T(8,128)(2,1)}, bf16[800,128]{1,0:T(8,128)(2,1)}) custom-call(s32[2]{0:T(128)} %pad_add_fusion.place_ref, s32[1,2]{1,0:T(1,128)} %near_ref.1, s32[1,1024]{1,0:T(1,128)} %slots_ref.1, bf16[512,128]{1,0:T(8,128)(2,1)} %keys_ref.1, bf16[512,128]{1,0:T(8,128)(2,1)} %values_ref.1, bf16[512,128]{1,0:T(8,128)(2,1)} %queries_ref.1), custom_call_target="tpu_custom_call" | custom-call | tf_op jit(solution)/shard_map/units/units/pallas_call | solution.py:96
  5.7 2.2 %collective-permute-start = (bf16[800,128]{1,0:T(8,128)(2,1)}, bf16[800,128]{1,0:T(8,128)(2,1)S(1)}, u32[]{:S(2)}, u32[]{:S(2)}) collective-permute-start(bf16[800,128]{1,0:T(8,128)(2,1)} %get-tuple-element.33), channel_id=1, source_target_pairs={{0,4},{4,0},{8,12},{12,8},{16,20},{20,16},{24,28},{28,24},{32,36},... | collective-permute-start | bytes 614408 | tf_op jit(solution)/shard_map/gather_keys/ppermute | solution.py:24
  7.8 1.0 slice.115
  9.8 4.1 %collective-permute-done.mate_ref = bf16[800,128]{1,0:T(8,128)(2,1)S(1)} collective-permute-done((bf16[800,128]{1,0:T(8,128)(2,1)}, bf16[800,128]{1,0:T(8,128)(2,1)S(1)}, u32[]{:S(2)}, u32[]{:S(2)}) %collective-permute-start) | collective-permute-done | bytes 204832 | tf_op jit(solution)/shard_map/gather_keys/ppermute | solution.py:24
  14.0 1.0 copy-done.2
  15.0 9.7 %collective-permute-start.2 = (bf16[1344,128]{1,0:T(8,128)(2,1)S(1)}, bf16[1344,128]{1,0:T(8,128)(2,1)S(1)}, u32[]{:S(2)}, u32[]{:S(2)}) collective-permute-start(bf16[1344,128]{1,0:T(8,128)(2,1)S(1)} %pad_maximum_fusion.1), channel_id=1, source_target_pairs={{0,248},{4,252},{8,0},{12,4},{16,8},{20,12},{24,16},{28,20},{32,24... | collective-permute-start | bytes 1032200 | tf_op jit(solution)/shard_map/gather_keys/ppermute | solution.py:24
  24.7 1.1 collective-permute-start.3
  27.3 7.2 %collective-permute-start.8 = (bf16[256,128]{1,0:T(8,128)(2,1)S(1)}, bf16[256,128]{1,0:T(8,128)(2,1)S(1)}, u32[]{:S(2)}, u32[]{:S(2)}) collective-permute-start(bf16[256,128]{1,0:T(8,128)(2,1)S(1)} %get-tuple-element.62), channel_id=1, source_target_pairs={{0,248},{4,252},{8,0},{12,4},{16,8},{20,12},{24,16},{28,20},{32,24... | collective-permute-start | bytes 196616 | tf_op jit(solution)/shard_map/cotangent/ppermute | solution.py:24
  34.6 5.0 %collective-permute-done.8.cot_rim = bf16[256,128]{1,0:T(8,128)(2,1)S(1)} collective-permute-done((bf16[256,128]{1,0:T(8,128)(2,1)S(1)}, bf16[256,128]{1,0:T(8,128)(2,1)S(1)}, u32[]{:S(2)}, u32[]{:S(2)}) %collective-permute-start.8) | collective-permute-done | bytes 65568 | tf_op jit(solution)/shard_map/cotangent/ppermute | solution.py:24
  39.7 1.0 collective-permute-start.9
  40.7 25.0 %attention_backward.1 = (bf16[1024,128]{1,0:T(8,128)(2,1)}, bf16[1280,128]{1,0:T(8,128)(2,1)}, bf16[512,128]{1,0:T(8,128)(2,1)}, f32[2,768,128]{2,1,0:T(8,128)},...) custom-call(s32[1]{0:T(128)} %bitcast.member_ref, ...), custom_call_target="tpu_custom_call" | custom-call | flops 20000000000 | bytes 4000000 | tf_op jit(solution)/shard_map/attention/attention_backward/pallas_call | solution.py:268
  65.8 8.0 %collective-permute-start.12 = (bf16[1024,128]{1,0:T(8,128)(2,1)}, bf16[1024,128]{1,0:T(8,128)(2,1)S(1)}, u32[]{:S(2)}, u32[]{:S(2)}) collective-permute-start(bf16[1024,128]{1,0:T(8,128)(2,1)} %get-tuple-element.51), channel_id=1, source_target_pairs={{0,248},{4,252},{8,0},{12,4},{16,8},{20,12},{24,16},{28,20},{32,24... | collective-permute-start | bytes 786440 | tf_op jit(solution)/shard_map/return_attention/ppermute | solution.py:24
  73.8 2.4 %collective-permute-done.10 = bf16[256,128]{1,0:T(8,128)(2,1)S(1)} collective-permute-done((bf16[256,128]{1,0:T(8,128)(2,1)}, bf16[256,128]{1,0:T(8,128)(2,1)S(1)}, u32[]{:S(2)}, u32[]{:S(2)}) %collective-permute-start.10) | collective-permute-done | bytes 65568 | tf_op jit(solution)/shard_map/return_attention/ppermute | solution.py:24
  76.2 1.0 fusion.11
  77.9 0.9 fusion
  78.8 3.5 %all-to-all-start = ((f32[8,8,512]{2,1,0:T(8,128)}), f32[8,8,512]{2,1,0:T(8,128)S(1)}, u32[]{:S(2)}, u32[]{:S(2)}) async-start(f32[8,8,512]{2,1,0:T(8,128)} %fusion), calls=%async_computation | async-start | bytes 262144 | tf_op jit(solution)/shard_map/w_out_grad/all_to_all | solution.py:365
  82.3 1.9 %collective-permute-start.13 = (bf16[512,128]{1,0:T(8,128)(2,1)S(1)}, bf16[512,128]{1,0:T(8,128)(2,1)S(1)}, u32[]{:S(2)}, u32[]{:S(2)}) collective-permute-start(bf16[512,128]{1,0:T(8,128)(2,1)S(1)} %copy-done.8), channel_id=1, source_target_pairs={{0,16},{4,20},{8,24},{12,28},{16,32},{20,36},{24,40},{28,44},{32,4... | collective-permute-start | bytes 393224 | tf_op jit(solution)/shard_map/return_attention/ppermute | solution.py:24
  84.2 7.0 %collective-permute-done.13 = bf16[512,128]{1,0:T(8,128)(2,1)S(1)} collective-permute-done((bf16[512,128]{1,0:T(8,128)(2,1)S(1)}, bf16[512,128]{1,0:T(8,128)(2,1)S(1)}, u32[]{:S(2)}, u32[]{:S(2)}) %collective-permute-start.13) | collective-permute-done | bytes 131104 | tf_op jit(solution)/shard_map/return_attention/ppermute | solution.py:24
  92.1 7.8 %all-to-all-start.1 = ((f32[8,8,512]{2,1,0:T(8,128)}), f32[8,8,512]{2,1,0:T(8,128)S(1)}, u32[]{:S(2)}, u32[]{:S(2)}) async-start(f32[8,8,512]{2,1,0:T(8,128)} %broadcast_in_dim.4), calls=%async_computation.1 | async-start | bytes 262144 | tf_op jit(solution)/shard_map/totals/all_to_all | solution.py:365
  100.0 1.1 copy-done.1
  101.2 5.3 %all-to-all-done.1 = f32[8,8,512]{2,1,0:T(8,128)S(1)} async-done(((f32[8,8,512]{2,1,0:T(8,128)}), f32[8,8,512]{2,1,0:T(8,128)S(1)}, u32[]{:S(2)}, u32[]{:S(2)}) %all-to-all-start.1) | async-done | bytes 131104 | tf_op jit(solution)/shard_map/totals/all_to_all | solution.py:365
  108.4 4.3 %all-to-all-start.2 = ((bf16[8,16,512]{2,1,0:T(8,128)(2,1)}), bf16[8,16,512]{2,1,0:T(8,128)(2,1)S(1)}, u32[]{:S(2)}, u32[]{:S(2)}) async-start(bf16[8,16,512]{2,1,0:T(8,128)(2,1)} %broadcast_in_dim.5), calls=%async_computation.2 | async-start | bytes 262144 | tf_op jit(solution)/shard_map/totals/all_to_all | solution.py:365
  114.3 7.5 %all-to-all-done.2 = bf16[8,16,512]{2,1,0:T(8,128)(2,1)S(1)} async-done(((bf16[8,16,512]{2,1,0:T(8,128)(2,1)}), bf16[8,16,512]{2,1,0:T(8,128)(2,1)S(1)}, u32[]{:S(2)}, u32[]{:S(2)}) %all-to-all-start.2) | async-done | bytes 131104 | tf_op jit(solution)/shard_map/totals/all_to_all | solution.py:365
  (72 shorter events, 9.8 us)
Async XLA Ops:
  0.6 8.3 %copy-start = (bf16[128,512]{1,0:T(8,128)(2,1)S(1)}, bf16[128,512]{1,0:T(8,128)(2,1)}, u32[]{:S(2)}) copy-start(bf16[128,512]{1,0:T(8,128)(2,1)} %param.11) | copy-start | bytes 393220
  0.6 8.2 %collective-permute-start.5 = (bf16[512,128]{1,0:T(8,128)(2,1)}, bf16[512,128]{1,0:T(8,128)(2,1)S(1)}, u32[]{:S(2)}, u32[]{:S(2)}) collective-permute-start(bf16[512,128]{1,0:T(8,128)(2,1)} %param.10), channel_id=1, source_target_pairs={{0,2},{1,3},{2,0},{3,1},{4,6},{5,7},{6,4},{7,5},{8,10},{9,11},{10,... | collective-permute-start | bytes 393224 | tf_op jit(solution)/shard_map/cotangent/ppermute | solution.py:328
  2.2 6.6 %collective-permute-start.4 = (bf16[512,128]{1,0:T(8,128)(2,1)}, bf16[512,128]{1,0:T(8,128)(2,1)S(1)}, u32[]{:S(2)}, u32[]{:S(2)}) collective-permute-start(bf16[512,128]{1,0:T(8,128)(2,1)} %param.10), channel_id=1, source_target_pairs={{0,3},{1,2},{2,1},{3,0},{4,7},{5,6},{6,5},{7,4},{8,11},{9,10},{10,... | collective-permute-start | bytes 393224 | tf_op jit(solution)/shard_map/cotangent/ppermute | solution.py:328
  2.2 6.6 %collective-permute-start.6 = (bf16[512,128]{1,0:T(8,128)(2,1)}, bf16[512,128]{1,0:T(8,128)(2,1)S(1)}, u32[]{:S(2)}, u32[]{:S(2)}) collective-permute-start(bf16[512,128]{1,0:T(8,128)(2,1)} %param.10), channel_id=1, source_target_pairs={{0,1},{1,0},{2,3},{3,2},{4,5},{5,4},{6,7},{7,6},{8,9},{9,8},{10,11... | collective-permute-start | bytes 393224 | tf_op jit(solution)/shard_map/cotangent/ppermute | solution.py:328
  5.7 8.3 %collective-permute-start = (bf16[800,128]{1,0:T(8,128)(2,1)}, bf16[800,128]{1,0:T(8,128)(2,1)S(1)}, u32[]{:S(2)}, u32[]{:S(2)}) collective-permute-start(bf16[800,128]{1,0:T(8,128)(2,1)} %get-tuple-element.33), channel_id=1, source_target_pairs={{0,4},{4,0},{8,12},{12,8},{16,20},{20,16},{24,28},{28,24},{32,36},... | collective-permute-start | bytes 614408 | tf_op jit(solution)/shard_map/gather_keys/ppermute | solution.py:24
  9.5 17.1 %collective-permute-start.7 = (bf16[256,128]{1,0:T(8,128)(2,1)S(1)}, bf16[256,128]{1,0:T(8,128)(2,1)S(1)}, u32[]{:S(2)}, u32[]{:S(2)}) collective-permute-start(bf16[256,128]{1,0:T(8,128)(2,1)S(1)} %broadcast_select_fusion.11), channel_id=1, source_target_pairs={{0,4},{4,0},{8,12},{12,8},{16,20},{20,16},{24,28},{28,24},{32,36},... | collective-permute-start | bytes 196616 | tf_op jit(solution)/shard_map/cotangent/ppermute | solution.py:24
  13.9 10.7 %copy-start.3 = (bf16[800,128]{1,0:T(8,128)(2,1)}, bf16[800,128]{1,0:T(8,128)(2,1)S(1)}, u32[]{:S(2)}) copy-start(bf16[800,128]{1,0:T(8,128)(2,1)S(1)} %collective-permute-done.mate_ref) | copy-start | bytes 614404
  15.0 24.7 %collective-permute-start.2 = (bf16[1344,128]{1,0:T(8,128)(2,1)S(1)}, bf16[1344,128]{1,0:T(8,128)(2,1)S(1)}, u32[]{:S(2)}, u32[]{:S(2)}) collective-permute-start(bf16[1344,128]{1,0:T(8,128)(2,1)S(1)} %pad_maximum_fusion.1), channel_id=1, source_target_pairs={{0,248},{4,252},{8,0},{12,4},{16,8},{20,12},{24,16},{28,20},{32,24... | collective-permute-start | bytes 1032200 | tf_op jit(solution)/shard_map/gather_keys/ppermute | solution.py:24
  24.7 14.9 %collective-permute-start.3 = (bf16[512,128]{1,0:T(8,128)(2,1)S(1)}, bf16[512,128]{1,0:T(8,128)(2,1)S(1)}, u32[]{:S(2)}, u32[]{:S(2)}) collective-permute-start(bf16[512,128]{1,0:T(8,128)(2,1)S(1)} %slice_select_fusion), channel_id=1, source_target_pairs={{0,240},{4,244},{8,248},{12,252},{16,0},{20,4},{24,8},{28,12},{32,... | collective-permute-start | bytes 393224 | tf_op jit(solution)/shard_map/gather_keys/ppermute | solution.py:24
  25.8 13.9 %collective-permute-start.1 = (bf16[1088,128]{1,0:T(8,128)(2,1)S(1)}, bf16[1088,128]{1,0:T(8,128)(2,1)S(1)}, u32[]{:S(2)}, u32[]{:S(2)}) collective-permute-start(bf16[1088,128]{1,0:T(8,128)(2,1)S(1)} %pad_maximum_fusion.2), channel_id=1, source_target_pairs={{0,8},{4,12},{8,16},{12,20},{16,24},{20,28},{24,32},{28,36},{32,40... | collective-permute-start | bytes 835592 | tf_op jit(solution)/shard_map/gather_keys/ppermute | solution.py:24
  27.3 12.3 %collective-permute-start.8 = (bf16[256,128]{1,0:T(8,128)(2,1)S(1)}, bf16[256,128]{1,0:T(8,128)(2,1)S(1)}, u32[]{:S(2)}, u32[]{:S(2)}) collective-permute-start(bf16[256,128]{1,0:T(8,128)(2,1)S(1)} %get-tuple-element.62), channel_id=1, source_target_pairs={{0,248},{4,252},{8,0},{12,4},{16,8},{20,12},{24,16},{28,20},{32,24... | collective-permute-start | bytes 196616 | tf_op jit(solution)/shard_map/cotangent/ppermute | solution.py:24
  39.6 1.0 copy-start.10
  39.6 1.0 copy-start.9
  39.7 26.0 %collective-permute-start.9 = (bf16[512,512]{1,0:T(8,128)(2,1)S(1)}, bf16[512,512]{1,0:T(8,128)(2,1)S(1)}, u32[]{:S(2)}, u32[]{:S(2)}) collective-permute-start(bf16[512,512]{1,0:T(8,128)(2,1)S(1)} %pad_maximum_fusion), channel_id=1, source_target_pairs={{0,4},{4,0},{8,12},{12,8},{16,20},{20,16},{24,28},{28,24},{32,36},... | collective-permute-start | bytes 1572872 | tf_op jit(solution)/shard_map/attention/ppermute | solution.py:24
  65.7 10.6 %collective-permute-start.10 = (bf16[256,128]{1,0:T(8,128)(2,1)}, bf16[256,128]{1,0:T(8,128)(2,1)S(1)}, u32[]{:S(2)}, u32[]{:S(2)}) collective-permute-start(bf16[256,128]{1,0:T(8,128)(2,1)} %get-tuple-element.47), channel_id=1, source_target_pairs={{0,8},{4,12},{8,16},{12,20},{16,24},{20,28},{24,32},{28,36},{32,40... | collective-permute-start | bytes 196616 | tf_op jit(solution)/shard_map/return_attention/ppermute | solution.py:24
  65.8 25.4 %collective-permute-start.12 = (bf16[1024,128]{1,0:T(8,128)(2,1)}, bf16[1024,128]{1,0:T(8,128)(2,1)S(1)}, u32[]{:S(2)}, u32[]{:S(2)}) collective-permute-start(bf16[1024,128]{1,0:T(8,128)(2,1)} %get-tuple-element.51), channel_id=1, source_target_pairs={{0,248},{4,252},{8,0},{12,4},{16,8},{20,12},{24,16},{28,20},{32,24... | collective-permute-start | bytes 786440 | tf_op jit(solution)/shard_map/return_attention/ppermute | solution.py:24
  73.8 17.5 %collective-permute-start.11 = (bf16[1280,128]{1,0:T(8,128)(2,1)}, bf16[1280,128]{1,0:T(8,128)(2,1)S(1)}, u32[]{:S(2)}, u32[]{:S(2)}) collective-permute-start(bf16[1280,128]{1,0:T(8,128)(2,1)} %get-tuple-element.50), channel_id=1, source_target_pairs={{0,8},{4,12},{8,16},{12,20},{16,24},{20,28},{24,32},{28,36},{32,40... | collective-permute-start | bytes 983048 | tf_op jit(solution)/shard_map/return_attention/ppermute | solution.py:24
  78.8 3.5 %copy-start.8 = (bf16[512,128]{1,0:T(8,128)(2,1)S(1)}, bf16[512,128]{1,0:T(8,128)(2,1)}, u32[]{:S(2)}) copy-start(bf16[512,128]{1,0:T(8,128)(2,1)} %get-tuple-element.52) | copy-start | bytes 393220
  78.8 12.5 %all-to-all-start = ((f32[8,8,512]{2,1,0:T(8,128)}), f32[8,8,512]{2,1,0:T(8,128)S(1)}, u32[]{:S(2)}, u32[]{:S(2)}) async-start(f32[8,8,512]{2,1,0:T(8,128)} %fusion), calls=%async_computation | async-start | bytes 262144 | tf_op jit(solution)/shard_map/w_out_grad/all_to_all | solution.py:365
  82.3 8.9 %collective-permute-start.13 = (bf16[512,128]{1,0:T(8,128)(2,1)S(1)}, bf16[512,128]{1,0:T(8,128)(2,1)S(1)}, u32[]{:S(2)}, u32[]{:S(2)}) collective-permute-start(bf16[512,128]{1,0:T(8,128)(2,1)S(1)} %copy-done.8), channel_id=1, source_target_pairs={{0,16},{4,20},{8,24},{12,28},{16,32},{20,36},{24,40},{28,44},{32,4... | collective-permute-start | bytes 393224 | tf_op jit(solution)/shard_map/return_attention/ppermute | solution.py:24
  92.1 14.5 %all-to-all-start.1 = ((f32[8,8,512]{2,1,0:T(8,128)}), f32[8,8,512]{2,1,0:T(8,128)S(1)}, u32[]{:S(2)}, u32[]{:S(2)}) async-start(f32[8,8,512]{2,1,0:T(8,128)} %broadcast_in_dim.4), calls=%async_computation.1 | async-start | bytes 262144 | tf_op jit(solution)/shard_map/totals/all_to_all | solution.py:365
  99.9 1.1 copy-start.1
  101.1 6.1 %collective-permute-start.14 = (bf16[768,128]{1,0:T(8,128)(2,1)S(1)}, bf16[768,128]{1,0:T(8,128)(2,1)S(1)}, u32[]{:S(2)}, u32[]{:S(2)}) collective-permute-start(bf16[768,128]{1,0:T(8,128)(2,1)S(1)} %select_convert_fusion), channel_id=1, source_target_pairs={{0,4},{4,0},{8,12},{12,8},{16,20},{20,16},{24,28},{28,24},{32,36},... | collective-permute-start | bytes 589832 | tf_op jit(solution)/shard_map/totals/ppermute | solution.py:24
  108.4 13.4 %all-to-all-start.2 = ((bf16[8,16,512]{2,1,0:T(8,128)(2,1)}), bf16[8,16,512]{2,1,0:T(8,128)(2,1)S(1)}, u32[]{:S(2)}, u32[]{:S(2)}) async-start(bf16[8,16,512]{2,1,0:T(8,128)(2,1)} %broadcast_in_dim.5), calls=%async_computation.2 | async-start | bytes 262144 | tf_op jit(solution)/shard_map/totals/all_to_all | solution.py:365
  (5 other events, 4.7 us)

commit v3 on v2

--- a/solution.py
+++ b/solution.py
@@ -12,7 +12,6 @@
 TILE = 256
 META = 32
 UNIT = BLK + META
-FULL = UNIT + HALF
 F32 = jnp.float32
 BF16 = jnp.bfloat16
 ABSENT = -1e30
@@ -38,9 +37,11 @@
     return lax.broadcasted_iota(jnp.int32, (rows, 2 * HD), 1)
 
 
-def units_kernel(place_ref, near_ref, slots_ref, keys_ref, values_ref, queries_ref, own, theirs):
-    place = place_ref[0]
-    blocks = place_ref[1]
+def units_kernel(
+    near_ref, slots_ref, keys_ref, values_ref, queries_ref, own, theirs, own_rows, their_rows
+):
+    place = lax.axis_index("blk")
+    blocks = lax.axis_size("blk")
     slots = slots_ref[...] - place * BLK
     slots = jnp.where(slots < 0, slots + blocks * BLK, slots)
     high = lax.broadcasted_iota(jnp.int32, (16, 2 * BLK), 0)
@@ -69,42 +70,46 @@
     left = lanes(BLK) < HD
     short = lanes(HALF) < HD
 
-    def put(out, j):
+    def put(out, rows_out, j):
         if j == 0:
             out[0:BLK, :] = jnp.where(left, keys, rolled(values))
-            out[UNIT:FULL, :] = jnp.where(short, top, rolled(end))
+            rows_out[...] = jnp.where(short, top, rolled(end))
         else:
             out[0:BLK, :] = jnp.where(left, rolled(keys), values)
-            out[UNIT:FULL, :] = jnp.where(short, rolled(top), end)
+            rows_out[...] = jnp.where(short, rolled(top), end)
         out[BLK:UNIT, :] = meta
 
     @pl.when(lax.rem(place, 2) == 0)
     def _():
-        put(own, 0)
-        put(theirs, 1)
+        put(own, own_rows, 0)
+        put(theirs, their_rows, 1)
 
     @pl.when(lax.rem(place, 2) == 1)
     def _():
-        put(own, 1)
-        put(theirs, 0)
+        put(own, own_rows, 1)
+        put(theirs, their_rows, 0)
 
 
 def make_units(*operands):
     smem = pl.BlockSpec(memory_space=pltpu.SMEM)
     vmem = pl.BlockSpec(memory_space=pltpu.VMEM)
-    unit = jax.ShapeDtypeStruct((FULL, 2 * HD), BF16)
+    unit = jax.ShapeDtypeStruct((UNIT, 2 * HD), BF16)
+    rows = jax.ShapeDtypeStruct((HALF, 2 * HD), BF16)
     return pl.pallas_call(
         units_kernel,
-        out_shape=(unit, unit),
-        in_specs=[smem, smem] + [vmem] * 4,
-        out_specs=(vmem, vmem),
+        out_shape=(unit, unit, rows, rows),
+        in_specs=[smem] + [vmem] * 4,
+        out_specs=(vmem,) * 4,
         name="units",
     )(*operands)
 
 
 def forward_prepare(
-    member, own_ref, mate_ref, left_ref, right_ref, last_ref, kv, query, meta, bias, weight
+    place, own_ref, mate_ref, across_ref, beyond_ref, last_ref, kv, meta, bias, weight
 ):
+    member = lax.rem(place, 2)
+    upper = lax.rem(place, 4) // 2
+
     def put_keys(slot, rows):
         kv[pl.ds(pl.multiple_of(slot * BLK, BLK), BLK), :] = rows
 
@@ -115,24 +120,11 @@
         at = member if far == 0 else 1 - member
         put_keys(2 + at, near[0:BLK, :])
         put_meta(2 + at, near[BLK:UNIT, :])
-        for first, pair in ((0, left_ref), (4, right_ref)):
+        for first, pair in ((4 - 4 * upper, across_ref), (4 * upper, beyond_ref)):
             base = far * UNIT
             put_keys(first + at, pair[base : base + BLK, :])
             put_meta(first + at, pair[base + BLK : base + UNIT, :])
     put_keys(6, last_ref[...])
-
-    def put_query(slot, rows):
-        scaled = rows * 0.125
-        zero = jnp.zeros_like(scaled)
-        at = pl.multiple_of(slot * BLK, BLK)
-        low = lanes(HALF) < HD
-        flipped = pltpu.roll(scaled.astype(F32), HD, 1).astype(BF16)
-        query[pl.ds(at, HALF), :] = jnp.where(low, scaled, zero)
-        query[pl.ds(at + HALF, HALF), :] = jnp.where(low, flipped, zero)
-
-    put_query(member, own_ref[UNIT:FULL, :])
-    put_query(1 - member, mate_ref[UNIT:FULL, :])
-    put_query(2, right_ref[2 * UNIT : 2 * UNIT + HALF, :])
 
     def counts(patch):
         rows = meta[patch * META : (patch + 1) * META, :].astype(F32)
@@ -171,26 +163,34 @@
 
 
 def attention_kernel(
-    member_ref, own_ref, mate_ref, left_ref, right_ref, last_ref, cot_own, cot_mate, cot_rim,
+    own_ref, mate_ref, across_ref, beyond_ref, last_ref,
+    own_rows, mate_rows, rim_rows,
     left_out, right_out, last_out, pair_out, mine_out, mate_out, rim_out,
     kv, query, cot, meta, bias, weight, kv_acc, row_acc,
 ):
-    member = member_ref[0]
+    place = lax.axis_index("blk")
+    member = lax.rem(place, 2)
     forward_prepare(
-        member, own_ref, mate_ref, left_ref, right_ref, last_ref, kv, query, meta, bias, weight
+        place, own_ref, mate_ref, across_ref, beyond_ref, last_ref, kv, meta, bias, weight
     )
 
     def put(slot, rows):
-        zero = jnp.zeros_like(rows)
         at = pl.multiple_of(slot * BLK, BLK)
         high = lanes(HALF) >= HD
-        flipped = pltpu.roll(rows.astype(F32), HD, 1).astype(BF16)
-        cot[pl.ds(at, HALF), :] = jnp.where(high, flipped, zero)
-        cot[pl.ds(at + HALF, HALF), :] = jnp.where(high, rows, zero)
-
-    put(member, cot_own[...])
-    put(1 - member, cot_mate[...])
-    put(2, cot_rim[...])
+
+        def unfold(out, part, start, keep):
+            zero = jnp.zeros_like(part)
+            other = pltpu.roll(part.astype(F32), HD, 1).astype(BF16)
+            first, second = (other, part) if start else (part, other)
+            out[pl.ds(at, HALF), :] = jnp.where(keep, first, zero)
+            out[pl.ds(at + HALF, HALF), :] = jnp.where(keep, second, zero)
+
+        unfold(query, rows[0:HALF, :] * 0.125, 0, ~high)
+        unfold(cot, rows[HALF:BLK, :], 1, high)
+
+    put(member, own_rows)
+    put(1 - member, mate_rows)
+    put(2, rim_rows)
     kv_acc[...] = jnp.zeros_like(kv_acc)
     row_acc[...] = jnp.zeros_like(row_acc)
 
@@ -205,33 +205,34 @@
         def softmax(job):
             peak = jnp.max(scores[job], axis=1, keepdims=True)
             grown = jnp.exp(scores[job] - peak)
-            probs = grown * (times[job] / jnp.sum(grown, axis=1, keepdims=True))
-            return probs, probs.astype(BF16)
-
-        def score_grads(job, probs, attn, d_probs):
+            share = times[job] / jnp.sum(grown, axis=1, keepdims=True)
+            return share, grown.astype(BF16)
+
+        def score_grads(job, share, low, attn, d_probs):
             delta = jnp.sum(attn * d[job].astype(F32), axis=1, keepdims=True)
             delta = delta / jnp.maximum(times[job], 1.0)
-            return (probs * (d_probs - delta)).astype(BF16)
-
-        def gather_grads(job, low, attn, d_scores):
+            return (low.astype(F32) * ((d_probs - delta) * share)).astype(BF16)
+
+        def gather_grads(job, share, low, attn, d_scores):
+            shared = (d[job].astype(F32) * share).astype(BF16)
             d_query = contract(d_scores, keys[job], 1, 0) * 0.125
             row_acc[rows[job], :] += jnp.where(lanes(TILE) < HD, d_query, attn)
             first = job * BLK
             kv_acc[:, first : first + WIN] += contract(q[job], d_scores, 0, 0) + contract(
-                d[job], low, 0, 0
+                shared, low, 0, 0
             )
 
         scores = [contract(q[job], keys[job], 1, 1) + bias[job] for job in range(2)]
-        probs_a, low_a = softmax(0)
+        share_a, low_a = softmax(0)
         d_probs_a = contract(d[0], keys[0], 1, 1)
-        attn_a = contract(low_a, keys[0], 1, 0)
-        probs_b, low_b = softmax(1)
-        d_scores_a = score_grads(0, probs_a, attn_a, d_probs_a)
+        attn_a = contract(low_a, keys[0], 1, 0) * share_a
+        share_b, low_b = softmax(1)
+        d_scores_a = score_grads(0, share_a, low_a, attn_a, d_probs_a)
         d_probs_b = contract(d[1], keys[1], 1, 1)
-        attn_b = contract(low_b, keys[1], 1, 0)
-        gather_grads(0, low_a, attn_a, d_scores_a)
-        d_scores_b = score_grads(1, probs_b, attn_b, d_probs_b)
-        gather_grads(1, low_b, attn_b, d_scores_b)
+        attn_b = contract(low_b, keys[1], 1, 0) * share_b
+        gather_grads(0, share_a, low_a, attn_a, d_scores_a)
+        d_scores_b = score_grads(1, share_b, low_b, attn_b, d_probs_b)
+        gather_grads(1, share_b, low_b, attn_b, d_scores_b)
         return carry
 
     lax.fori_loop(0, 2 * BLK // TILE, step, 0)
@@ -274,7 +275,7 @@
             jax.ShapeDtypeStruct((2, BLK + HALF, 2 * HD), F32),
             *[jax.ShapeDtypeStruct((HALF, 2 * HD), BF16)] * 3,
         ),
-        in_specs=[pl.BlockSpec(memory_space=pltpu.SMEM)] + [vmem] * 8,
+        in_specs=[vmem] * 8,
         out_specs=(vmem,) * 7,
         scratch_shapes=[
             pltpu.VMEM((7 * BLK, 2 * HD), BF16),
@@ -299,7 +300,6 @@
     blocks = lax.axis_size("blk")
     member = lax.rem(place, 2)
     second = member == 1
-    flag = jnp.reshape(member, (1,)).astype(jnp.int32)
 
     def pick(if_first, if_second):
         return jnp.where(second, if_second, if_first)
@@ -311,15 +311,15 @@
         return array[:, j * HD : (j + 1) * HD]
 
     with jax.named_scope("units"):
-        where = jnp.stack([place, jnp.full_like(place, blocks)]).astype(jnp.int32)
-        own, theirs = make_units(where, neighbours, slot_point, keys, values, queries)
+        own, theirs, own_rows, their_rows = make_units(
+            neighbours, slot_point, keys, values, queries
+        )
 
     with jax.named_scope("gather_keys"):
         mate = swap(theirs, 1)
-        rim_query = pick(own[UNIT:], mate[UNIT:])
-        pair = jnp.concatenate([own[:UNIT], mate[:UNIT], rim_query])
-        left = send(pair[: 2 * UNIT], lambda i: i + 2)
-        right = send(pair, lambda i: i - 2)
+        pair = jnp.concatenate([own, mate])
+        across = swap(pair, 2)
+        beyond = send(across, lambda i: i + 4 if i % 4 < 2 else i - 4)
         last = send(pick(own[:BLK], mate[:BLK]), lambda i: i - 4)
 
     with jax.named_scope("cotangent"):
@@ -335,17 +335,17 @@
         )
         d_attn = jnp.dot(grad_all, w_out.T, preferred_element_type=F32).astype(BF16)
         cots = [folded(of_head(d_attn, j)) for j in range(2)]
-        cot_own = pick(cots[0], cots[1])
-        cot_mate = swap(pick(cots[1], cots[0]), 1)
-        cot_rim = send(pick(cot_own, cot_mate), lambda i: i - 2)
+        rows_own = jnp.concatenate([own_rows, pick(cots[0], cots[1])])
+        rows_mate = swap(jnp.concatenate([their_rows, pick(cots[1], cots[0])]), 1)
+        rows_rim = send(pick(rows_own, rows_mate), lambda i: i - 2)
 
     with jax.named_scope("attention"):
-        left, right, last, cot_rim, grad_sent = lax.optimization_barrier(
-            (left, right, last, cot_rim, grad_all)
+        across, beyond, last, rows_rim, grad_sent = lax.optimization_barrier(
+            (across, beyond, last, rows_rim, grad_all)
         )
         grad_mate = swap(grad_sent, 1)
         left_grad, right_grad, last_grad, pair_grad, mine, theirs, rim = attention(
-            flag, own, mate, left, right, last, cot_own, cot_mate, cot_rim
+            own, mate, across, beyond, last, rows_own, rows_mate, rows_rim
         )
         left_grad, right_grad, last_grad, pair_grad, mine, theirs, rim, grad_mate = (
             lax.optimization_barrier(
@@ -392,9 +392,10 @@
         w_part = part(mine, grad_all, 0) + part(mine, grad_all, 1)
         w_part = w_part + part(theirs, grad_mate, 0) + part(theirs, grad_mate, 1)
         around = exchange(w_part, planes)
-        around, from_left, from_right, from_last = lax.optimization_barrier(
-            (around, from_left, from_right, from_last)
-        )
+        width = around.shape[1]
+        around = jnp.sum(around.reshape(8, HD // 8, width), axis=0)
+        around = exchange(copies(around), others)
+        around = jnp.sum(around.reshape(4, HD // 4, width), axis=0).astype(BF16)
 
     with jax.named_scope("totals"):
         from_left = from_left.astype(F32)
@@ -406,13 +407,10 @@
             [from_left[BLK : 2 * BLK] + from_right[BLK:], jnp.zeros((HALF, 2 * HD), F32)]
         )
         mine = pick(first, other)
-        got = swap(pick(other, first).astype(BF16), 1)
-        width = around.shape[1]
-        around = jnp.sum(around.reshape(8, HD // 8, width), axis=0)
-        around = exchange(copies(around), others)
-        around = jnp.sum(around.reshape(4, HD // 4, width), axis=0).astype(BF16)
-        around, got = lax.optimization_barrier((around, got))
-        around = exchange(copies(around), planes)
+        to_mate = pick(other, first).astype(BF16)
+        around, to_mate = lax.optimization_barrier((copies(around), to_mate))
+        got = swap(to_mate, 1)
+        around = exchange(around, planes)
         around = jnp.swapaxes(around.reshape(8, 2, HD // 8, width), 0, 1)
         w_grad = around.reshape(2 * HD, width).astype(F32)
         heads = [pick(mine, got.astype(F32)), pick(got.astype(F32), mine)]

time: 123 us -> 119 us (0.967)
  starting transfers between devices: 50.2 us -> 54.8 us
  waiting for transfers between devices: 32.2 us -> 27.7 us
  local copies, waits for them, and re-layouts: 5.53 us -> 3.6 us
  Pallas kernels: 27.2 us -> 25.9 us
    ppermute x12, waiting for transfers between devices: 19.2 us -> 8.24 us  [send(): return lax.ppermute(block, 'blk', route)]
    all_to_all x3, waiting for transfers between devices: 13 us -> 18.5 us  [exchange(): lax.all_to_all(rows, 'blk', 0, 0, axis_index_groups=groups, tiled=True)]
    ppermute x12, starting transfers between devices: 32.4 us -> 37.1 us  [send(): return lax.ppermute(block, 'blk', route)]
    pallas_call x1, Pallas kernels: 25 us -> 23.7 us  [attention(): pl.pallas_call(attention_kernel, out_shape=(jax.ShapeDtypeStruct((2 * BLK...]
where the time goes in v3:
time: 119 us
  starting transfers between devices  54.8 us (46%)
  waiting for transfers between devices  27.7 us (23%)
  Pallas kernels  25.9 us (22%)
  other arithmetic  3.96 us (3%)
  local copies, waits for them, and re-layouts  3.6 us (3%)
  matrix products  1.83 us (2%)
    ppermute x12, starting transfers between devices, send(): return lax.ppermute(block, 'blk', route)  37.1 us
    pallas_call x1, Pallas kernels, attention(): pl.pallas_call(attention_kernel, out_shape=(jax.ShapeDtypeStruct((2 * BLK...  23.7 us
    all_to_all x3, waiting for transfers between devices, exchange(): lax.all_to_all(rows, 'blk', 0, 0, axis_index_groups=groups, tiled=True)  18.5 us
    all_to_all x3, starting transfers between devices, exchange(): lax.all_to_all(rows, 'blk', 0, 0, axis_index_groups=groups, tiled=True)  15.5 us
    ppermute x12, waiting for transfers between devices, send(): return lax.ppermute(block, 'blk', route)  8.24 us
  transfers between devices with their start and end apart: 18, of which 8 were waited for; matrix products, arithmetic and copies ran while one was open for 6% of the time, Pallas kernels for 22%

profile of v3, /device:TPU:8, one launch (start us, length us, event | category | flops | bytes accessed | tf_op | source)
XLA Modules:
  0.0 118.6 jit_solution(10450311520306097565)
XLA Ops:
  0.7 1.6 %collective-permute-start.5 = (bf16[512,128]{1,0:T(8,128)(2,1)}, bf16[512,128]{1,0:T(8,128)(2,1)S(1)}, u32[]{:S(2)}, u32[]{:S(2)}) collective-permute-start(bf16[512,128]{1,0:T(8,128)(2,1)} %param.10), channel_id=1, source_target_pairs={{0,2},{1,3},{2,0},{3,1},{4,6},{5,7},{6,4},{7,5},{8,10},{9,11},{10,... | collective-permute-start | bytes 393224 | tf_op jit(solution)/shard_map/cotangent/ppermute | solution.py:328
  2.9 2.2 %units.1 = (bf16[544,128]{1,0:T(8,128)(2,1)}, bf16[544,128]{1,0:T(8,128)(2,1)}, bf16[256,128]{1,0:T(8,128)(2,1)}, bf16[256,128]{1,0:T(8,128)(2,1)}) custom-call(s32[1,2]{1,0:T(1,128)} %near_ref.1, s32[1,1024]{1,0:T(1,128)} %slots_ref.1, bf16[512,128]{1,0:T(8,128)(2,1)} %keys_ref.1, bf16[512,128]{1,0:T(8,128)(2,1)} %values_ref.1, bf16[512,128]{1,0:T(8,128)(2,1)} %queries_ref.1), custom_call_target="tpu_custom_call" | custom-call | tf_op jit(solution)/shard_map/units/units/pallas_call | solution.py:98
  5.1 2.2 %collective-permute-start = (bf16[544,128]{1,0:T(8,128)(2,1)}, bf16[544,128]{1,0:T(8,128)(2,1)S(1)}, u32[]{:S(2)}, u32[]{:S(2)}) collective-permute-start(bf16[544,128]{1,0:T(8,128)(2,1)} %get-tuple-element.31), channel_id=1, source_target_pairs={{0,4},{4,0},{8,12},{12,8},{16,20},{20,16},{24,28},{28,24},{32,36},... | collective-permute-start | bytes 417800 | tf_op jit(solution)/shard_map/gather_keys/ppermute | solution.py:23
  8.9 2.4 %collective-permute-done.mate_ref = bf16[544,128]{1,0:T(8,128)(2,1)S(1)} collective-permute-done((bf16[544,128]{1,0:T(8,128)(2,1)}, bf16[544,128]{1,0:T(8,128)(2,1)S(1)}, u32[]{:S(2)}, u32[]{:S(2)}) %collective-permute-start) | collective-permute-done | bytes 139296 | tf_op jit(solution)/shard_map/gather_keys/ppermute | solution.py:23
  11.3 1.9 %collective-permute-start.1 = (bf16[1088,128]{1,0:T(8,128)(2,1)S(1)}, bf16[1088,128]{1,0:T(8,128)(2,1)S(1)}, u32[]{:S(2)}, u32[]{:S(2)}) collective-permute-start(bf16[1088,128]{1,0:T(8,128)(2,1)S(1)} %pad_maximum_fusion.1), channel_id=1, source_target_pairs={{0,8},{4,12},{8,0},{12,4},{16,24},{20,28},{24,16},{28,20},{32,40},... | collective-permute-start | bytes 835592 | tf_op jit(solution)/shard_map/gather_keys/ppermute | solution.py:23
  13.3 1.4 %collective-permute-start.7 = (bf16[512,128]{1,0:T(8,128)(2,1)S(1)}, bf16[512,128]{1,0:T(8,128)(2,1)S(1)}, u32[]{:S(2)}, u32[]{:S(2)}) collective-permute-start(bf16[512,128]{1,0:T(8,128)(2,1)S(1)} %pad_maximum_fusion.2), channel_id=1, source_target_pairs={{0,4},{4,0},{8,12},{12,8},{16,20},{20,16},{24,28},{28,24},{32,36},... | collective-permute-start | bytes 393224 | tf_op jit(solution)/shard_map/cotangent/ppermute | solution.py:23
  14.8 8.4 %collective-permute-start.3 = (bf16[512,128]{1,0:T(8,128)(2,1)S(1)}, bf16[512,128]{1,0:T(8,128)(2,1)S(1)}, u32[]{:S(2)}, u32[]{:S(2)}) collective-permute-start(bf16[512,128]{1,0:T(8,128)(2,1)S(1)} %slice_select_fusion), channel_id=1, source_target_pairs={{0,240},{4,244},{8,248},{12,252},{16,0},{20,4},{24,8},{28,12},{32,... | collective-permute-start | bytes 393224 | tf_op jit(solution)/shard_map/gather_keys/ppermute | solution.py:23
  24.7 9.1 %collective-permute-start.8 = (bf16[512,128]{1,0:T(8,128)(2,1)S(1)}, bf16[512,128]{1,0:T(8,128)(2,1)S(1)}, u32[]{:S(2)}, u32[]{:S(2)}) collective-permute-start(bf16[512,128]{1,0:T(8,128)(2,1)S(1)} %get-tuple-element.75), channel_id=1, source_target_pairs={{0,248},{4,252},{8,0},{12,4},{16,8},{20,12},{24,16},{28,20},{32,24... | collective-permute-start | bytes 393224 | tf_op jit(solution)/shard_map/cotangent/ppermute | solution.py:23
  33.8 2.5 %collective-permute-done.8.rim_rows = bf16[512,128]{1,0:T(8,128)(2,1)S(1)} collective-permute-done((bf16[512,128]{1,0:T(8,128)(2,1)S(1)}, bf16[512,128]{1,0:T(8,128)(2,1)S(1)}, u32[]{:S(2)}, u32[]{:S(2)}) %collective-permute-start.8) | collective-permute-done | bytes 131104 | tf_op jit(solution)/shard_map/cotangent/ppermute | solution.py:23
  36.4 1.6 %collective-permute-start.9 = (bf16[512,512]{1,0:T(8,128)(2,1)S(1)}, bf16[512,512]{1,0:T(8,128)(2,1)S(1)}, u32[]{:S(2)}, u32[]{:S(2)}) collective-permute-start(bf16[512,512]{1,0:T(8,128)(2,1)S(1)} %pad_maximum_fusion), channel_id=1, source_target_pairs={{0,4},{4,0},{8,12},{12,8},{16,20},{20,16},{24,28},{28,24},{32,36},... | collective-permute-start | bytes 1572872 | tf_op jit(solution)/shard_map/attention/ppermute | solution.py:23
  38.0 23.7 %attention_backward.1 = (bf16[1024,128]{1,0:T(8,128)(2,1)}, bf16[1280,128]{1,0:T(8,128)(2,1)}, bf16[512,128]{1,0:T(8,128)(2,1)}, f32[2,768,128]{2,1,0:T(8,128)},...) custom-call(bf16[544,128]{1,0:T(8,128)(2,1)} %get-tuple-element.30.own_ref, ...), custom_call_target="tpu_custom_call" | custom-call | flops 20000000000 | bytes 4000000 | tf_op jit(solution)/shard_map/attention/attention_backward/pallas_call | solution.py:269
  61.6 4.0 %collective-permute-start.10 = (bf16[256,128]{1,0:T(8,128)(2,1)}, bf16[256,128]{1,0:T(8,128)(2,1)S(1)}, u32[]{:S(2)}, u32[]{:S(2)}) collective-permute-start(bf16[256,128]{1,0:T(8,128)(2,1)} %get-tuple-element.47), channel_id=1, source_target_pairs={{0,8},{4,12},{8,16},{12,20},{16,24},{20,28},{24,32},{28,36},{32,40... | collective-permute-start | bytes 196616 | tf_op jit(solution)/shard_map/return_attention/ppermute | solution.py:23
  65.6 4.1 %collective-permute-start.12 = (bf16[1024,128]{1,0:T(8,128)(2,1)}, bf16[1024,128]{1,0:T(8,128)(2,1)S(1)}, u32[]{:S(2)}, u32[]{:S(2)}) collective-permute-start(bf16[1024,128]{1,0:T(8,128)(2,1)} %get-tuple-element.52), channel_id=1, source_target_pairs={{0,248},{4,252},{8,0},{12,4},{16,8},{20,12},{24,16},{28,20},{32,24... | collective-permute-start | bytes 786440 | tf_op jit(solution)/shard_map/return_attention/ppermute | solution.py:23
  69.8 2.5 %collective-permute-done.10 = bf16[256,128]{1,0:T(8,128)(2,1)S(1)} collective-permute-done((bf16[256,128]{1,0:T(8,128)(2,1)}, bf16[256,128]{1,0:T(8,128)(2,1)S(1)}, u32[]{:S(2)}, u32[]{:S(2)}) %collective-permute-start.10) | collective-permute-done | bytes 65568 | tf_op jit(solution)/shard_map/return_attention/ppermute | solution.py:23
  72.3 1.0 fusion.11
  74.8 3.5 %all-to-all-start = ((f32[8,8,512]{2,1,0:T(8,128)}), f32[8,8,512]{2,1,0:T(8,128)S(1)}, u32[]{:S(2)}, u32[]{:S(2)}) async-start(f32[8,8,512]{2,1,0:T(8,128)} %fusion), calls=%async_computation | async-start | bytes 262144 | tf_op jit(solution)/shard_map/w_out_grad/all_to_all | solution.py:365
  78.4 1.9 %collective-permute-start.13 = (bf16[512,128]{1,0:T(8,128)(2,1)S(1)}, bf16[512,128]{1,0:T(8,128)(2,1)S(1)}, u32[]{:S(2)}, u32[]{:S(2)}) collective-permute-start(bf16[512,128]{1,0:T(8,128)(2,1)S(1)} %copy-done.10), channel_id=1, source_target_pairs={{0,16},{4,20},{8,24},{12,28},{16,32},{20,36},{24,40},{28,44},{32,4... | collective-permute-start | bytes 393224 | tf_op jit(solution)/shard_map/return_attention/ppermute | solution.py:23
  80.3 7.1 %all-to-all-done = f32[8,8,512]{2,1,0:T(8,128)S(1)} async-done(((f32[8,8,512]{2,1,0:T(8,128)}), f32[8,8,512]{2,1,0:T(8,128)S(1)}, u32[]{:S(2)}, u32[]{:S(2)}) %all-to-all-start) | async-done | bytes 131104 | tf_op jit(solution)/shard_map/w_out_grad/all_to_all | solution.py:365
  88.1 8.6 %all-to-all-start.1 = ((f32[8,8,512]{2,1,0:T(8,128)}), f32[8,8,512]{2,1,0:T(8,128)S(1)}, u32[]{:S(2)}, u32[]{:S(2)}) async-start(f32[8,8,512]{2,1,0:T(8,128)} %broadcast_in_dim.4), calls=%async_computation.1 | async-start | bytes 262144 | tf_op jit(solution)/shard_map/w_out_grad/all_to_all | solution.py:365
  96.9 1.0 copy-done.1
  98.0 5.3 %all-to-all-done.1 = f32[8,8,512]{2,1,0:T(8,128)S(1)} async-done(((f32[8,8,512]{2,1,0:T(8,128)}), f32[8,8,512]{2,1,0:T(8,128)S(1)}, u32[]{:S(2)}, u32[]{:S(2)}) %all-to-all-start.1) | async-done | bytes 131104 | tf_op jit(solution)/shard_map/w_out_grad/all_to_all | solution.py:365
  103.9 1.5 %collective-permute-start.14 = (bf16[768,128]{1,0:T(8,128)(2,1)S(1)}, bf16[768,128]{1,0:T(8,128)(2,1)S(1)}, u32[]{:S(2)}, u32[]{:S(2)}) collective-permute-start(bf16[768,128]{1,0:T(8,128)(2,1)S(1)} %select_convert_fusion), channel_id=1, source_target_pairs={{0,4},{4,0},{8,12},{12,8},{16,20},{20,16},{24,28},{28,24},{32,36},... | collective-permute-start | bytes 589832 | tf_op jit(solution)/shard_map/totals/ppermute | solution.py:23
  105.4 3.4 %all-to-all-start.2 = ((bf16[8,16,512]{2,1,0:T(8,128)(2,1)}), bf16[8,16,512]{2,1,0:T(8,128)(2,1)S(1)}, u32[]{:S(2)}, u32[]{:S(2)}) async-start(bf16[8,16,512]{2,1,0:T(8,128)(2,1)} %bitcast.5), calls=%async_computation.2 | async-start | bytes 262144 | tf_op jit(solution)/shard_map/totals/all_to_all | solution.py:365
  111.7 6.1 %all-to-all-done.2 = bf16[8,16,512]{2,1,0:T(8,128)(2,1)S(1)} async-done(((bf16[8,16,512]{2,1,0:T(8,128)(2,1)}), bf16[8,16,512]{2,1,0:T(8,128)(2,1)S(1)}, u32[]{:S(2)}, u32[]{:S(2)}) %all-to-all-start.2) | async-done | bytes 131104 | tf_op jit(solution)/shard_map/totals/all_to_all | solution.py:365
  (72 shorter events, 10.6 us)
Async XLA Ops:
  0.6 7.7 %copy-start = (bf16[128,512]{1,0:T(8,128)(2,1)S(1)}, bf16[128,512]{1,0:T(8,128)(2,1)}, u32[]{:S(2)}) copy-start(bf16[128,512]{1,0:T(8,128)(2,1)} %param.11) | copy-start | bytes 393220
  0.6 7.6 %copy-start.4 = (bf16[512,128]{1,0:T(8,128)(2,1)S(1)}, bf16[512,128]{1,0:T(8,128)(2,1)}, u32[]{:S(2)}) copy-start(bf16[512,128]{1,0:T(8,128)(2,1)} %param.10) | copy-start | bytes 393220
  0.7 6.6 %collective-permute-start.5 = (bf16[512,128]{1,0:T(8,128)(2,1)}, bf16[512,128]{1,0:T(8,128)(2,1)S(1)}, u32[]{:S(2)}, u32[]{:S(2)}) collective-permute-start(bf16[512,128]{1,0:T(8,128)(2,1)} %param.10), channel_id=1, source_target_pairs={{0,2},{1,3},{2,0},{3,1},{4,6},{5,7},{6,4},{7,5},{8,10},{9,11},{10,... | collective-permute-start | bytes 393224 | tf_op jit(solution)/shard_map/cotangent/ppermute | solution.py:328
  2.2 6.0 %collective-permute-start.4 = (bf16[512,128]{1,0:T(8,128)(2,1)}, bf16[512,128]{1,0:T(8,128)(2,1)S(1)}, u32[]{:S(2)}, u32[]{:S(2)}) collective-permute-start(bf16[512,128]{1,0:T(8,128)(2,1)} %param.10), channel_id=1, source_target_pairs={{0,3},{1,2},{2,1},{3,0},{4,7},{5,6},{6,5},{7,4},{8,11},{9,10},{10,... | collective-permute-start | bytes 393224 | tf_op jit(solution)/shard_map/cotangent/ppermute | solution.py:328
  2.2 6.0 %collective-permute-start.6 = (bf16[512,128]{1,0:T(8,128)(2,1)}, bf16[512,128]{1,0:T(8,128)(2,1)S(1)}, u32[]{:S(2)}, u32[]{:S(2)}) collective-permute-start(bf16[512,128]{1,0:T(8,128)(2,1)} %param.10), channel_id=1, source_target_pairs={{0,1},{1,0},{2,3},{3,2},{4,5},{5,4},{6,7},{7,6},{8,9},{9,8},{10,11... | collective-permute-start | bytes 393224 | tf_op jit(solution)/shard_map/cotangent/ppermute | solution.py:328
  5.1 6.2 %collective-permute-start = (bf16[544,128]{1,0:T(8,128)(2,1)}, bf16[544,128]{1,0:T(8,128)(2,1)S(1)}, u32[]{:S(2)}, u32[]{:S(2)}) collective-permute-start(bf16[544,128]{1,0:T(8,128)(2,1)} %get-tuple-element.31), channel_id=1, source_target_pairs={{0,4},{4,0},{8,12},{12,8},{16,20},{20,16},{24,28},{28,24},{32,36},... | collective-permute-start | bytes 417800 | tf_op jit(solution)/shard_map/gather_keys/ppermute | solution.py:23
  11.3 11.8 %collective-permute-start.1 = (bf16[1088,128]{1,0:T(8,128)(2,1)S(1)}, bf16[1088,128]{1,0:T(8,128)(2,1)S(1)}, u32[]{:S(2)}, u32[]{:S(2)}) collective-permute-start(bf16[1088,128]{1,0:T(8,128)(2,1)S(1)} %pad_maximum_fusion.1), channel_id=1, source_target_pairs={{0,8},{4,12},{8,0},{12,4},{16,24},{20,28},{24,16},{28,20},{32,40},... | collective-permute-start | bytes 835592 | tf_op jit(solution)/shard_map/gather_keys/ppermute | solution.py:23
  13.3 10.7 %copy-start.6 = (bf16[256,128]{1,0:T(8,128)(2,1)S(1)}, bf16[256,128]{1,0:T(8,128)(2,1)}, u32[]{:S(2)}) copy-start(bf16[256,128]{1,0:T(8,128)(2,1)} %get-tuple-element.33) | copy-start | bytes 196612
  13.3 10.7 %collective-permute-start.7 = (bf16[512,128]{1,0:T(8,128)(2,1)S(1)}, bf16[512,128]{1,0:T(8,128)(2,1)S(1)}, u32[]{:S(2)}, u32[]{:S(2)}) collective-permute-start(bf16[512,128]{1,0:T(8,128)(2,1)S(1)} %pad_maximum_fusion.2), channel_id=1, source_target_pairs={{0,4},{4,0},{8,12},{12,8},{16,20},{20,16},{24,28},{28,24},{32,36},... | collective-permute-start | bytes 393224 | tf_op jit(solution)/shard_map/cotangent/ppermute | solution.py:23
  14.8 19.1 %collective-permute-start.3 = (bf16[512,128]{1,0:T(8,128)(2,1)S(1)}, bf16[512,128]{1,0:T(8,128)(2,1)S(1)}, u32[]{:S(2)}, u32[]{:S(2)}) collective-permute-start(bf16[512,128]{1,0:T(8,128)(2,1)S(1)} %slice_select_fusion), channel_id=1, source_target_pairs={{0,240},{4,244},{8,248},{12,252},{16,0},{20,4},{24,8},{28,12},{32,... | collective-permute-start | bytes 393224 | tf_op jit(solution)/shard_map/gather_keys/ppermute | solution.py:23
  23.2 14.8 %copy-start.8 = (bf16[1088,128]{1,0:T(8,128)(2,1)}, bf16[1088,128]{1,0:T(8,128)(2,1)S(1)}, u32[]{:S(2)}) copy-start(bf16[1088,128]{1,0:T(8,128)(2,1)S(1)} %collective-permute-done.1.across_ref) | copy-start | bytes 835588
  23.2 13.2 %collective-permute-start.2 = (bf16[1088,128]{1,0:T(8,128)(2,1)S(1)}, bf16[1088,128]{1,0:T(8,128)(2,1)S(1)}, u32[]{:S(2)}, u32[]{:S(2)}) collective-permute-start(bf16[1088,128]{1,0:T(8,128)(2,1)S(1)} %collective-permute-done.1.across_ref), channel_id=1, source_target_pairs={{0,16},{4,20},{8,248},{12,252},{16,32},{20,36},{24,8},{28,12},{32,... | collective-permute-start | bytes 835592 | tf_op jit(solution)/shard_map/gather_keys/ppermute | solution.py:23
  24.7 11.7 %collective-permute-start.8 = (bf16[512,128]{1,0:T(8,128)(2,1)S(1)}, bf16[512,128]{1,0:T(8,128)(2,1)S(1)}, u32[]{:S(2)}, u32[]{:S(2)}) collective-permute-start(bf16[512,128]{1,0:T(8,128)(2,1)S(1)} %get-tuple-element.75), channel_id=1, source_target_pairs={{0,248},{4,252},{8,0},{12,4},{16,8},{20,12},{24,16},{28,20},{32,24... | collective-permute-start | bytes 393224 | tf_op jit(solution)/shard_map/cotangent/ppermute | solution.py:23
  33.8 4.1 %copy-start.11 = (bf16[512,128]{1,0:T(8,128)(2,1)}, bf16[512,128]{1,0:T(8,128)(2,1)S(1)}, u32[]{:S(2)}) copy-start(bf16[512,128]{1,0:T(8,128)(2,1)S(1)} %collective-permute-done.3.last_ref) | copy-start | bytes 393220
  36.4 25.3 %collective-permute-start.9 = (bf16[512,512]{1,0:T(8,128)(2,1)S(1)}, bf16[512,512]{1,0:T(8,128)(2,1)S(1)}, u32[]{:S(2)}, u32[]{:S(2)}) collective-permute-start(bf16[512,512]{1,0:T(8,128)(2,1)S(1)} %pad_maximum_fusion), channel_id=1, source_target_pairs={{0,4},{4,0},{8,12},{12,8},{16,20},{20,16},{24,28},{28,24},{32,36},... | collective-permute-start | bytes 1572872 | tf_op jit(solution)/shard_map/attention/ppermute | solution.py:23
  61.6 10.7 %collective-permute-start.10 = (bf16[256,128]{1,0:T(8,128)(2,1)}, bf16[256,128]{1,0:T(8,128)(2,1)S(1)}, u32[]{:S(2)}, u32[]{:S(2)}) collective-permute-start(bf16[256,128]{1,0:T(8,128)(2,1)} %get-tuple-element.47), channel_id=1, source_target_pairs={{0,8},{4,12},{8,16},{12,20},{16,24},{20,28},{24,32},{28,36},{32,40... | collective-permute-start | bytes 196616 | tf_op jit(solution)/shard_map/return_attention/ppermute | solution.py:23
  65.6 14.7 %collective-permute-start.12 = (bf16[1024,128]{1,0:T(8,128)(2,1)}, bf16[1024,128]{1,0:T(8,128)(2,1)S(1)}, u32[]{:S(2)}, u32[]{:S(2)}) collective-permute-start(bf16[1024,128]{1,0:T(8,128)(2,1)} %get-tuple-element.52), channel_id=1, source_target_pairs={{0,248},{4,252},{8,0},{12,4},{16,8},{20,12},{24,16},{28,20},{32,24... | collective-permute-start | bytes 786440 | tf_op jit(solution)/shard_map/return_attention/ppermute | solution.py:23
  69.8 26.9 %collective-permute-start.11 = (bf16[1280,128]{1,0:T(8,128)(2,1)}, bf16[1280,128]{1,0:T(8,128)(2,1)S(1)}, u32[]{:S(2)}, u32[]{:S(2)}) collective-permute-start(bf16[1280,128]{1,0:T(8,128)(2,1)} %get-tuple-element.51), channel_id=1, source_target_pairs={{0,8},{4,12},{8,16},{12,20},{16,24},{20,28},{24,32},{28,36},{32,40... | collective-permute-start | bytes 983048 | tf_op jit(solution)/shard_map/return_attention/ppermute | solution.py:23
  74.8 3.5 %copy-start.10 = (bf16[512,128]{1,0:T(8,128)(2,1)S(1)}, bf16[512,128]{1,0:T(8,128)(2,1)}, u32[]{:S(2)}) copy-start(bf16[512,128]{1,0:T(8,128)(2,1)} %get-tuple-element.53) | copy-start | bytes 393220
  74.8 12.5 %all-to-all-start = ((f32[8,8,512]{2,1,0:T(8,128)}), f32[8,8,512]{2,1,0:T(8,128)S(1)}, u32[]{:S(2)}, u32[]{:S(2)}) async-start(f32[8,8,512]{2,1,0:T(8,128)} %fusion), calls=%async_computation | async-start | bytes 262144 | tf_op jit(solution)/shard_map/w_out_grad/all_to_all | solution.py:365
  78.4 18.4 %collective-permute-start.13 = (bf16[512,128]{1,0:T(8,128)(2,1)S(1)}, bf16[512,128]{1,0:T(8,128)(2,1)S(1)}, u32[]{:S(2)}, u32[]{:S(2)}) collective-permute-start(bf16[512,128]{1,0:T(8,128)(2,1)S(1)} %copy-done.10), channel_id=1, source_target_pairs={{0,16},{4,20},{8,24},{12,28},{16,32},{20,36},{24,40},{28,44},{32,4... | collective-permute-start | bytes 393224 | tf_op jit(solution)/shard_map/return_attention/ppermute | solution.py:23
  88.1 15.2 %all-to-all-start.1 = ((f32[8,8,512]{2,1,0:T(8,128)}), f32[8,8,512]{2,1,0:T(8,128)S(1)}, u32[]{:S(2)}, u32[]{:S(2)}) async-start(f32[8,8,512]{2,1,0:T(8,128)} %broadcast_in_dim.4), calls=%async_computation.1 | async-start | bytes 262144 | tf_op jit(solution)/shard_map/w_out_grad/all_to_all | solution.py:365
  103.9 5.7 %collective-permute-start.14 = (bf16[768,128]{1,0:T(8,128)(2,1)S(1)}, bf16[768,128]{1,0:T(8,128)(2,1)S(1)}, u32[]{:S(2)}, u32[]{:S(2)}) collective-permute-start(bf16[768,128]{1,0:T(8,128)(2,1)S(1)} %select_convert_fusion), channel_id=1, source_target_pairs={{0,4},{4,0},{8,12},{12,8},{16,20},{20,16},{24,28},{28,24},{32,36},... | collective-permute-start | bytes 589832 | tf_op jit(solution)/shard_map/totals/ppermute | solution.py:23
  105.4 12.4 %all-to-all-start.2 = ((bf16[8,16,512]{2,1,0:T(8,128)(2,1)}), bf16[8,16,512]{2,1,0:T(8,128)(2,1)S(1)}, u32[]{:S(2)}, u32[]{:S(2)}) async-start(bf16[8,16,512]{2,1,0:T(8,128)(2,1)} %bitcast.5), calls=%async_computation.2 | async-start | bytes 262144 | tf_op jit(solution)/shard_map/totals/all_to_all | solution.py:365
  (7 other events, 13.0 us)

commit v4 on v3

--- a/solution.py
+++ b/solution.py
@@ -9,7 +9,7 @@
 BLK = 512
 HALF = BLK // 2
 WIN = 6 * BLK
-TILE = 256
+TILE = 512
 META = 32
 UNIT = BLK + META
 F32 = jnp.float32

time: 119 us -> 119 us (level)
  transfers between devices with their start and end apart: 18 -> 18, of which waited for: 8 -> 8; matrix products, arithmetic and copies ran while one was open for 6% -> 6% of each run, Pallas kernels for 22% -> 21%
where the time goes in v4:
time: 119 us; the launch traced here: 118 us
  starting transfers between devices  55 us (46%)
  waiting for transfers between devices  27.5 us (23%)
  Pallas kernels  25.3 us (21%)
  other arithmetic  3.96 us (3%)
  local copies, waits for them, and re-layouts  3.6 us (3%)
  matrix products  1.83 us (2%)
    ppermute x12, starting transfers between devices, send(): return lax.ppermute(block, 'blk', route)  37.3 us
    pallas_call x1, Pallas kernels, attention(): pl.pallas_call(attention_kernel, out_shape=(jax.ShapeDtypeStruct((2 * BLK...  23.1 us
    all_to_all x3, waiting for transfers between devices, exchange(): lax.all_to_all(rows, 'blk', 0, 0, axis_index_groups=groups, tiled=True)  18.5 us
    all_to_all x3, starting transfers between devices, exchange(): lax.all_to_all(rows, 'blk', 0, 0, axis_index_groups=groups, tiled=True)  15.5 us
    ppermute x12, waiting for transfers between devices, send(): return lax.ppermute(block, 'blk', route)  8.03 us
  transfers between devices with their start and end apart: 18, of which 8 were waited for; matrix products, arithmetic and copies ran while one was open for 6% of the time, Pallas kernels for 21%

profile of v4, /device:TPU:8, one launch (start us, length us, event | category | flops | bytes accessed | tf_op | source)
XLA Modules:
  0.0 118.0 jit_solution(13426291215621683761)
XLA Ops:
  0.7 1.6 %collective-permute-start.5 = (bf16[512,128]{1,0:T(8,128)(2,1)}, bf16[512,128]{1,0:T(8,128)(2,1)S(1)}, u32[]{:S(2)}, u32[]{:S(2)}) collective-permute-start(bf16[512,128]{1,0:T(8,128)(2,1)} %param.10), channel_id=1, source_target_pairs={{0,2},{1,3},{2,0},{3,1},{4,6},{5,7},{6,4},{7,5},{8,10},{9,11},{10,... | collective-permute-start | bytes 393224 | tf_op jit(solution)/shard_map/cotangent/ppermute | solution.py:328
  2.9 2.2 %units.1 = (bf16[544,128]{1,0:T(8,128)(2,1)}, bf16[544,128]{1,0:T(8,128)(2,1)}, bf16[256,128]{1,0:T(8,128)(2,1)}, bf16[256,128]{1,0:T(8,128)(2,1)}) custom-call(s32[1,2]{1,0:T(1,128)} %near_ref.1, s32[1,1024]{1,0:T(1,128)} %slots_ref.1, bf16[512,128]{1,0:T(8,128)(2,1)} %keys_ref.1, bf16[512,128]{1,0:T(8,128)(2,1)} %values_ref.1, bf16[512,128]{1,0:T(8,128)(2,1)} %queries_ref.1), custom_call_target="tpu_custom_call" | custom-call | tf_op jit(solution)/shard_map/units/units/pallas_call | solution.py:98
  5.1 2.2 %collective-permute-start = (bf16[544,128]{1,0:T(8,128)(2,1)}, bf16[544,128]{1,0:T(8,128)(2,1)S(1)}, u32[]{:S(2)}, u32[]{:S(2)}) collective-permute-start(bf16[544,128]{1,0:T(8,128)(2,1)} %get-tuple-element.31), channel_id=1, source_target_pairs={{0,4},{4,0},{8,12},{12,8},{16,20},{20,16},{24,28},{28,24},{32,36},... | collective-permute-start | bytes 417800 | tf_op jit(solution)/shard_map/gather_keys/ppermute | solution.py:23
  8.9 2.4 %collective-permute-done.mate_ref = bf16[544,128]{1,0:T(8,128)(2,1)S(1)} collective-permute-done((bf16[544,128]{1,0:T(8,128)(2,1)}, bf16[544,128]{1,0:T(8,128)(2,1)S(1)}, u32[]{:S(2)}, u32[]{:S(2)}) %collective-permute-start) | collective-permute-done | bytes 139296 | tf_op jit(solution)/shard_map/gather_keys/ppermute | solution.py:23
  11.3 1.9 %collective-permute-start.1 = (bf16[1088,128]{1,0:T(8,128)(2,1)S(1)}, bf16[1088,128]{1,0:T(8,128)(2,1)S(1)}, u32[]{:S(2)}, u32[]{:S(2)}) collective-permute-start(bf16[1088,128]{1,0:T(8,128)(2,1)S(1)} %pad_maximum_fusion.1), channel_id=1, source_target_pairs={{0,8},{4,12},{8,0},{12,4},{16,24},{20,28},{24,16},{28,20},{32,40},... | collective-permute-start | bytes 835592 | tf_op jit(solution)/shard_map/gather_keys/ppermute | solution.py:23
  13.3 1.4 %collective-permute-start.7 = (bf16[512,128]{1,0:T(8,128)(2,1)S(1)}, bf16[512,128]{1,0:T(8,128)(2,1)S(1)}, u32[]{:S(2)}, u32[]{:S(2)}) collective-permute-start(bf16[512,128]{1,0:T(8,128)(2,1)S(1)} %pad_maximum_fusion.2), channel_id=1, source_target_pairs={{0,4},{4,0},{8,12},{12,8},{16,20},{20,16},{24,28},{28,24},{32,36},... | collective-permute-start | bytes 393224 | tf_op jit(solution)/shard_map/cotangent/ppermute | solution.py:23
  14.8 8.4 %collective-permute-start.3 = (bf16[512,128]{1,0:T(8,128)(2,1)S(1)}, bf16[512,128]{1,0:T(8,128)(2,1)S(1)}, u32[]{:S(2)}, u32[]{:S(2)}) collective-permute-start(bf16[512,128]{1,0:T(8,128)(2,1)S(1)} %slice_select_fusion), channel_id=1, source_target_pairs={{0,240},{4,244},{8,248},{12,252},{16,0},{20,4},{24,8},{28,12},{32,... | collective-permute-start | bytes 393224 | tf_op jit(solution)/shard_map/gather_keys/ppermute | solution.py:23
  24.7 9.1 %collective-permute-start.8 = (bf16[512,128]{1,0:T(8,128)(2,1)S(1)}, bf16[512,128]{1,0:T(8,128)(2,1)S(1)}, u32[]{:S(2)}, u32[]{:S(2)}) collective-permute-start(bf16[512,128]{1,0:T(8,128)(2,1)S(1)} %get-tuple-element.75), channel_id=1, source_target_pairs={{0,248},{4,252},{8,0},{12,4},{16,8},{20,12},{24,16},{28,20},{32,24... | collective-permute-start | bytes 393224 | tf_op jit(solution)/shard_map/cotangent/ppermute | solution.py:23
  33.8 2.5 %collective-permute-done.8.rim_rows = bf16[512,128]{1,0:T(8,128)(2,1)S(1)} collective-permute-done((bf16[512,128]{1,0:T(8,128)(2,1)S(1)}, bf16[512,128]{1,0:T(8,128)(2,1)S(1)}, u32[]{:S(2)}, u32[]{:S(2)}) %collective-permute-start.8) | collective-permute-done | bytes 131104 | tf_op jit(solution)/shard_map/cotangent/ppermute | solution.py:23
  36.4 1.6 %collective-permute-start.9 = (bf16[512,512]{1,0:T(8,128)(2,1)S(1)}, bf16[512,512]{1,0:T(8,128)(2,1)S(1)}, u32[]{:S(2)}, u32[]{:S(2)}) collective-permute-start(bf16[512,512]{1,0:T(8,128)(2,1)S(1)} %pad_maximum_fusion), channel_id=1, source_target_pairs={{0,4},{4,0},{8,12},{12,8},{16,20},{20,16},{24,28},{28,24},{32,36},... | collective-permute-start | bytes 1572872 | tf_op jit(solution)/shard_map/attention/ppermute | solution.py:23
  38.0 23.1 %attention_backward.1 = (bf16[1024,128]{1,0:T(8,128)(2,1)}, bf16[1280,128]{1,0:T(8,128)(2,1)}, bf16[512,128]{1,0:T(8,128)(2,1)}, f32[2,768,128]{2,1,0:T(8,128)},...) custom-call(bf16[544,128]{1,0:T(8,128)(2,1)} %get-tuple-element.30.own_ref, ...), custom_call_target="tpu_custom_call" | custom-call | flops 20000000000 | bytes 4000000 | tf_op jit(solution)/shard_map/attention/attention_backward/pallas_call | solution.py:269
  61.1 4.0 %collective-permute-start.10 = (bf16[256,128]{1,0:T(8,128)(2,1)}, bf16[256,128]{1,0:T(8,128)(2,1)S(1)}, u32[]{:S(2)}, u32[]{:S(2)}) collective-permute-start(bf16[256,128]{1,0:T(8,128)(2,1)} %get-tuple-element.47), channel_id=1, source_target_pairs={{0,8},{4,12},{8,16},{12,20},{16,24},{20,28},{24,32},{28,36},{32,40... | collective-permute-start | bytes 196616 | tf_op jit(solution)/shard_map/return_attention/ppermute | solution.py:23
  65.1 4.4 %collective-permute-start.12 = (bf16[1024,128]{1,0:T(8,128)(2,1)}, bf16[1024,128]{1,0:T(8,128)(2,1)S(1)}, u32[]{:S(2)}, u32[]{:S(2)}) collective-permute-start(bf16[1024,128]{1,0:T(8,128)(2,1)} %get-tuple-element.52), channel_id=1, source_target_pairs={{0,248},{4,252},{8,0},{12,4},{16,8},{20,12},{24,16},{28,20},{32,24... | collective-permute-start | bytes 786440 | tf_op jit(solution)/shard_map/return_attention/ppermute | solution.py:23
  69.4 2.3 %collective-permute-done.10 = bf16[256,128]{1,0:T(8,128)(2,1)S(1)} collective-permute-done((bf16[256,128]{1,0:T(8,128)(2,1)}, bf16[256,128]{1,0:T(8,128)(2,1)S(1)}, u32[]{:S(2)}, u32[]{:S(2)}) %collective-permute-start.10) | collective-permute-done | bytes 65568 | tf_op jit(solution)/shard_map/return_attention/ppermute | solution.py:23
  71.7 1.0 fusion.11
  74.3 3.5 %all-to-all-start = ((f32[8,8,512]{2,1,0:T(8,128)}), f32[8,8,512]{2,1,0:T(8,128)S(1)}, u32[]{:S(2)}, u32[]{:S(2)}) async-start(f32[8,8,512]{2,1,0:T(8,128)} %fusion), calls=%async_computation | async-start | bytes 262144 | tf_op jit(solution)/shard_map/w_out_grad/all_to_all | solution.py:365
  77.8 1.9 %collective-permute-start.13 = (bf16[512,128]{1,0:T(8,128)(2,1)S(1)}, bf16[512,128]{1,0:T(8,128)(2,1)S(1)}, u32[]{:S(2)}, u32[]{:S(2)}) collective-permute-start(bf16[512,128]{1,0:T(8,128)(2,1)S(1)} %copy-done.10), channel_id=1, source_target_pairs={{0,16},{4,20},{8,24},{12,28},{16,32},{20,36},{24,40},{28,44},{32,4... | collective-permute-start | bytes 393224 | tf_op jit(solution)/shard_map/return_attention/ppermute | solution.py:23
  79.8 7.1 %all-to-all-done = f32[8,8,512]{2,1,0:T(8,128)S(1)} async-done(((f32[8,8,512]{2,1,0:T(8,128)}), f32[8,8,512]{2,1,0:T(8,128)S(1)}, u32[]{:S(2)}, u32[]{:S(2)}) %all-to-all-start) | async-done | bytes 131104 | tf_op jit(solution)/shard_map/w_out_grad/all_to_all | solution.py:365
  87.5 8.6 %all-to-all-start.1 = ((f32[8,8,512]{2,1,0:T(8,128)}), f32[8,8,512]{2,1,0:T(8,128)S(1)}, u32[]{:S(2)}, u32[]{:S(2)}) async-start(f32[8,8,512]{2,1,0:T(8,128)} %broadcast_in_dim.4), calls=%async_computation.1 | async-start | bytes 262144 | tf_op jit(solution)/shard_map/w_out_grad/all_to_all | solution.py:365
  96.3 1.0 copy-done.1
  97.4 5.3 %all-to-all-done.1 = f32[8,8,512]{2,1,0:T(8,128)S(1)} async-done(((f32[8,8,512]{2,1,0:T(8,128)}), f32[8,8,512]{2,1,0:T(8,128)S(1)}, u32[]{:S(2)}, u32[]{:S(2)}) %all-to-all-start.1) | async-done | bytes 131104 | tf_op jit(solution)/shard_map/w_out_grad/all_to_all | solution.py:365
  103.4 1.5 %collective-permute-start.14 = (bf16[768,128]{1,0:T(8,128)(2,1)S(1)}, bf16[768,128]{1,0:T(8,128)(2,1)S(1)}, u32[]{:S(2)}, u32[]{:S(2)}) collective-permute-start(bf16[768,128]{1,0:T(8,128)(2,1)S(1)} %select_convert_fusion), channel_id=1, source_target_pairs={{0,4},{4,0},{8,12},{12,8},{16,20},{20,16},{24,28},{28,24},{32,36},... | collective-permute-start | bytes 589832 | tf_op jit(solution)/shard_map/totals/ppermute | solution.py:23
  104.9 3.4 %all-to-all-start.2 = ((bf16[8,16,512]{2,1,0:T(8,128)(2,1)}), bf16[8,16,512]{2,1,0:T(8,128)(2,1)S(1)}, u32[]{:S(2)}, u32[]{:S(2)}) async-start(bf16[8,16,512]{2,1,0:T(8,128)(2,1)} %bitcast.5), calls=%async_computation.2 | async-start | bytes 262144 | tf_op jit(solution)/shard_map/totals/all_to_all | solution.py:365
  111.2 6.1 %all-to-all-done.2 = bf16[8,16,512]{2,1,0:T(8,128)(2,1)S(1)} async-done(((bf16[8,16,512]{2,1,0:T(8,128)(2,1)}), bf16[8,16,512]{2,1,0:T(8,128)(2,1)S(1)}, u32[]{:S(2)}, u32[]{:S(2)}) %all-to-all-start.2) | async-done | bytes 131104 | tf_op jit(solution)/shard_map/totals/all_to_all | solution.py:365
  (72 shorter events, 10.6 us)
Async XLA Ops:
  0.6 7.7 %copy-start = (bf16[128,512]{1,0:T(8,128)(2,1)S(1)}, bf16[128,512]{1,0:T(8,128)(2,1)}, u32[]{:S(2)}) copy-start(bf16[128,512]{1,0:T(8,128)(2,1)} %param.11) | copy-start | bytes 393220
  0.6 7.6 %copy-start.4 = (bf16[512,128]{1,0:T(8,128)(2,1)S(1)}, bf16[512,128]{1,0:T(8,128)(2,1)}, u32[]{:S(2)}) copy-start(bf16[512,128]{1,0:T(8,128)(2,1)} %param.10) | copy-start | bytes 393220
  0.7 6.6 %collective-permute-start.5 = (bf16[512,128]{1,0:T(8,128)(2,1)}, bf16[512,128]{1,0:T(8,128)(2,1)S(1)}, u32[]{:S(2)}, u32[]{:S(2)}) collective-permute-start(bf16[512,128]{1,0:T(8,128)(2,1)} %param.10), channel_id=1, source_target_pairs={{0,2},{1,3},{2,0},{3,1},{4,6},{5,7},{6,4},{7,5},{8,10},{9,11},{10,... | collective-permute-start | bytes 393224 | tf_op jit(solution)/shard_map/cotangent/ppermute | solution.py:328
  2.2 6.0 %collective-permute-start.4 = (bf16[512,128]{1,0:T(8,128)(2,1)}, bf16[512,128]{1,0:T(8,128)(2,1)S(1)}, u32[]{:S(2)}, u32[]{:S(2)}) collective-permute-start(bf16[512,128]{1,0:T(8,128)(2,1)} %param.10), channel_id=1, source_target_pairs={{0,3},{1,2},{2,1},{3,0},{4,7},{5,6},{6,5},{7,4},{8,11},{9,10},{10,... | collective-permute-start | bytes 393224 | tf_op jit(solution)/shard_map/cotangent/ppermute | solution.py:328
  2.2 6.0 %collective-permute-start.6 = (bf16[512,128]{1,0:T(8,128)(2,1)}, bf16[512,128]{1,0:T(8,128)(2,1)S(1)}, u32[]{:S(2)}, u32[]{:S(2)}) collective-permute-start(bf16[512,128]{1,0:T(8,128)(2,1)} %param.10), channel_id=1, source_target_pairs={{0,1},{1,0},{2,3},{3,2},{4,5},{5,4},{6,7},{7,6},{8,9},{9,8},{10,11... | collective-permute-start | bytes 393224 | tf_op jit(solution)/shard_map/cotangent/ppermute | solution.py:328
  5.1 6.2 %collective-permute-start = (bf16[544,128]{1,0:T(8,128)(2,1)}, bf16[544,128]{1,0:T(8,128)(2,1)S(1)}, u32[]{:S(2)}, u32[]{:S(2)}) collective-permute-start(bf16[544,128]{1,0:T(8,128)(2,1)} %get-tuple-element.31), channel_id=1, source_target_pairs={{0,4},{4,0},{8,12},{12,8},{16,20},{20,16},{24,28},{28,24},{32,36},... | collective-permute-start | bytes 417800 | tf_op jit(solution)/shard_map/gather_keys/ppermute | solution.py:23
  11.3 11.8 %collective-permute-start.1 = (bf16[1088,128]{1,0:T(8,128)(2,1)S(1)}, bf16[1088,128]{1,0:T(8,128)(2,1)S(1)}, u32[]{:S(2)}, u32[]{:S(2)}) collective-permute-start(bf16[1088,128]{1,0:T(8,128)(2,1)S(1)} %pad_maximum_fusion.1), channel_id=1, source_target_pairs={{0,8},{4,12},{8,0},{12,4},{16,24},{20,28},{24,16},{28,20},{32,40},... | collective-permute-start | bytes 835592 | tf_op jit(solution)/shard_map/gather_keys/ppermute | solution.py:23
  13.3 10.7 %copy-start.6 = (bf16[256,128]{1,0:T(8,128)(2,1)S(1)}, bf16[256,128]{1,0:T(8,128)(2,1)}, u32[]{:S(2)}) copy-start(bf16[256,128]{1,0:T(8,128)(2,1)} %get-tuple-element.33) | copy-start | bytes 196612
  13.3 10.7 %collective-permute-start.7 = (bf16[512,128]{1,0:T(8,128)(2,1)S(1)}, bf16[512,128]{1,0:T(8,128)(2,1)S(1)}, u32[]{:S(2)}, u32[]{:S(2)}) collective-permute-start(bf16[512,128]{1,0:T(8,128)(2,1)S(1)} %pad_maximum_fusion.2), channel_id=1, source_target_pairs={{0,4},{4,0},{8,12},{12,8},{16,20},{20,16},{24,28},{28,24},{32,36},... | collective-permute-start | bytes 393224 | tf_op jit(solution)/shard_map/cotangent/ppermute | solution.py:23
  14.8 19.1 %collective-permute-start.3 = (bf16[512,128]{1,0:T(8,128)(2,1)S(1)}, bf16[512,128]{1,0:T(8,128)(2,1)S(1)}, u32[]{:S(2)}, u32[]{:S(2)}) collective-permute-start(bf16[512,128]{1,0:T(8,128)(2,1)S(1)} %slice_select_fusion), channel_id=1, source_target_pairs={{0,240},{4,244},{8,248},{12,252},{16,0},{20,4},{24,8},{28,12},{32,... | collective-permute-start | bytes 393224 | tf_op jit(solution)/shard_map/gather_keys/ppermute | solution.py:23
  23.2 14.8 %copy-start.8 = (bf16[1088,128]{1,0:T(8,128)(2,1)}, bf16[1088,128]{1,0:T(8,128)(2,1)S(1)}, u32[]{:S(2)}) copy-start(bf16[1088,128]{1,0:T(8,128)(2,1)S(1)} %collective-permute-done.1.across_ref) | copy-start | bytes 835588
  23.2 13.2 %collective-permute-start.2 = (bf16[1088,128]{1,0:T(8,128)(2,1)S(1)}, bf16[1088,128]{1,0:T(8,128)(2,1)S(1)}, u32[]{:S(2)}, u32[]{:S(2)}) collective-permute-start(bf16[1088,128]{1,0:T(8,128)(2,1)S(1)} %collective-permute-done.1.across_ref), channel_id=1, source_target_pairs={{0,16},{4,20},{8,248},{12,252},{16,32},{20,36},{24,8},{28,12},{32,... | collective-permute-start | bytes 835592 | tf_op jit(solution)/shard_map/gather_keys/ppermute | solution.py:23
  24.7 11.7 %collective-permute-start.8 = (bf16[512,128]{1,0:T(8,128)(2,1)S(1)}, bf16[512,128]{1,0:T(8,128)(2,1)S(1)}, u32[]{:S(2)}, u32[]{:S(2)}) collective-permute-start(bf16[512,128]{1,0:T(8,128)(2,1)S(1)} %get-tuple-element.75), channel_id=1, source_target_pairs={{0,248},{4,252},{8,0},{12,4},{16,8},{20,12},{24,16},{28,20},{32,24... | collective-permute-start | bytes 393224 | tf_op jit(solution)/shard_map/cotangent/ppermute | solution.py:23
  33.8 4.1 %copy-start.11 = (bf16[512,128]{1,0:T(8,128)(2,1)}, bf16[512,128]{1,0:T(8,128)(2,1)S(1)}, u32[]{:S(2)}) copy-start(bf16[512,128]{1,0:T(8,128)(2,1)S(1)} %collective-permute-done.3.last_ref) | copy-start | bytes 393220
  36.4 24.7 %collective-permute-start.9 = (bf16[512,512]{1,0:T(8,128)(2,1)S(1)}, bf16[512,512]{1,0:T(8,128)(2,1)S(1)}, u32[]{:S(2)}, u32[]{:S(2)}) collective-permute-start(bf16[512,512]{1,0:T(8,128)(2,1)S(1)} %pad_maximum_fusion), channel_id=1, source_target_pairs={{0,4},{4,0},{8,12},{12,8},{16,20},{20,16},{24,28},{28,24},{32,36},... | collective-permute-start | bytes 1572872 | tf_op jit(solution)/shard_map/attention/ppermute | solution.py:23
  61.1 10.7 %collective-permute-start.10 = (bf16[256,128]{1,0:T(8,128)(2,1)}, bf16[256,128]{1,0:T(8,128)(2,1)S(1)}, u32[]{:S(2)}, u32[]{:S(2)}) collective-permute-start(bf16[256,128]{1,0:T(8,128)(2,1)} %get-tuple-element.47), channel_id=1, source_target_pairs={{0,8},{4,12},{8,16},{12,20},{16,24},{20,28},{24,32},{28,36},{32,40... | collective-permute-start | bytes 196616 | tf_op jit(solution)/shard_map/return_attention/ppermute | solution.py:23
  65.1 14.7 %collective-permute-start.12 = (bf16[1024,128]{1,0:T(8,128)(2,1)}, bf16[1024,128]{1,0:T(8,128)(2,1)S(1)}, u32[]{:S(2)}, u32[]{:S(2)}) collective-permute-start(bf16[1024,128]{1,0:T(8,128)(2,1)} %get-tuple-element.52), channel_id=1, source_target_pairs={{0,248},{4,252},{8,0},{12,4},{16,8},{20,12},{24,16},{28,20},{32,24... | collective-permute-start | bytes 786440 | tf_op jit(solution)/shard_map/return_attention/ppermute | solution.py:23
  69.4 26.7 %collective-permute-start.11 = (bf16[1280,128]{1,0:T(8,128)(2,1)}, bf16[1280,128]{1,0:T(8,128)(2,1)S(1)}, u32[]{:S(2)}, u32[]{:S(2)}) collective-permute-start(bf16[1280,128]{1,0:T(8,128)(2,1)} %get-tuple-element.51), channel_id=1, source_target_pairs={{0,8},{4,12},{8,16},{12,20},{16,24},{20,28},{24,32},{28,36},{32,40... | collective-permute-start | bytes 983048 | tf_op jit(solution)/shard_map/return_attention/ppermute | solution.py:23
  74.3 3.5 %copy-start.10 = (bf16[512,128]{1,0:T(8,128)(2,1)S(1)}, bf16[512,128]{1,0:T(8,128)(2,1)}, u32[]{:S(2)}) copy-start(bf16[512,128]{1,0:T(8,128)(2,1)} %get-tuple-element.53) | copy-start | bytes 393220
  74.3 12.5 %all-to-all-start = ((f32[8,8,512]{2,1,0:T(8,128)}), f32[8,8,512]{2,1,0:T(8,128)S(1)}, u32[]{:S(2)}, u32[]{:S(2)}) async-start(f32[8,8,512]{2,1,0:T(8,128)} %fusion), calls=%async_computation | async-start | bytes 262144 | tf_op jit(solution)/shard_map/w_out_grad/all_to_all | solution.py:365
  77.8 18.4 %collective-permute-start.13 = (bf16[512,128]{1,0:T(8,128)(2,1)S(1)}, bf16[512,128]{1,0:T(8,128)(2,1)S(1)}, u32[]{:S(2)}, u32[]{:S(2)}) collective-permute-start(bf16[512,128]{1,0:T(8,128)(2,1)S(1)} %copy-done.10), channel_id=1, source_target_pairs={{0,16},{4,20},{8,24},{12,28},{16,32},{20,36},{24,40},{28,44},{32,4... | collective-permute-start | bytes 393224 | tf_op jit(solution)/shard_map/return_attention/ppermute | solution.py:23
  87.5 15.2 %all-to-all-start.1 = ((f32[8,8,512]{2,1,0:T(8,128)}), f32[8,8,512]{2,1,0:T(8,128)S(1)}, u32[]{:S(2)}, u32[]{:S(2)}) async-start(f32[8,8,512]{2,1,0:T(8,128)} %broadcast_in_dim.4), calls=%async_computation.1 | async-start | bytes 262144 | tf_op jit(solution)/shard_map/w_out_grad/all_to_all | solution.py:365
  103.4 5.7 %collective-permute-start.14 = (bf16[768,128]{1,0:T(8,128)(2,1)S(1)}, bf16[768,128]{1,0:T(8,128)(2,1)S(1)}, u32[]{:S(2)}, u32[]{:S(2)}) collective-permute-start(bf16[768,128]{1,0:T(8,128)(2,1)S(1)} %select_convert_fusion), channel_id=1, source_target_pairs={{0,4},{4,0},{8,12},{12,8},{16,20},{20,16},{24,28},{28,24},{32,36},... | collective-permute-start | bytes 589832 | tf_op jit(solution)/shard_map/totals/ppermute | solution.py:23
  104.9 12.4 %all-to-all-start.2 = ((bf16[8,16,512]{2,1,0:T(8,128)(2,1)}), bf16[8,16,512]{2,1,0:T(8,128)(2,1)S(1)}, u32[]{:S(2)}, u32[]{:S(2)}) async-start(bf16[8,16,512]{2,1,0:T(8,128)(2,1)} %bitcast.5), calls=%async_computation.2 | async-start | bytes 262144 | tf_op jit(solution)/shard_map/totals/all_to_all | solution.py:365
  (7 other events, 13.0 us)
